TPU v7x, 32 devices: a whole 2x2x4 slice. The times are simulated.
32 devices in a mesh: fsdp: 32 (over z, y, x, core).
Axes of the slice: x: 2, y: 2, z: 4, core: 2. Of those that a mesh axis runs over, the one named last changes fastest.
Arguments:
- tokens: bfloat16 [65536, 768], P('fsdp'), may hold values from -6 to 6
- mol_len: int32 [256], P('fsdp'), may hold values from 0 to 256, as said below
- cotangent: bfloat16 [65536, 768], P('fsdp'), may hold values from -6 to 6
- ln1_gain: bfloat16 [768], P('fsdp'), may hold values from 0.5 to 1.5
- ln1_bias: bfloat16 [768], P('fsdp'), may hold values from -1 to 1
- w_qkv: bfloat16 [768, 2304], P('fsdp'), may hold values from -0.21875 to 0.21875
- q_bias: bfloat16 [768], P('fsdp'), may hold values from -1 to 1
- v_bias: bfloat16 [768], P('fsdp'), may hold values from -1 to 1
- w_out: bfloat16 [768, 768], P('fsdp'), may hold values from -1.25 to 1.25
- out_bias: bfloat16 [768], P('fsdp'), may hold values from -1 to 1
- ln2_gain: bfloat16 [768], P('fsdp'), may hold values from 0.5 to 1.5
- ln2_bias: bfloat16 [768], P('fsdp'), may hold values from -1 to 1
- w_in: bfloat16 [768, 768], P('fsdp'), may hold values from -0.21875 to 0.21875
- in_bias: bfloat16 [768], P('fsdp'), may hold values from -1 to 1
- w_back: bfloat16 [768, 768], P('fsdp'), may hold values from -0.21875 to 0.21875
- back_bias: bfloat16 [768], P('fsdp'), may hold values from -1 to 1
Outputs:
- mixed_out: bfloat16 [65536, 768], P('fsdp')
- token_grad: bfloat16 [65536, 768], P('fsdp')
- grad_ln1_gain: float32 [768], P('fsdp')
- grad_ln1_bias: float32 [768], P('fsdp')
- grad_w_qkv: float32 [768, 2304], P('fsdp')
- grad_q_bias: float32 [768], P('fsdp')
- grad_v_bias: float32 [768], P('fsdp')
- grad_w_out: float32 [768, 768], P('fsdp')
- grad_out_bias: float32 [768], P('fsdp')
- grad_ln2_gain: float32 [768], P('fsdp')
- grad_ln2_bias: float32 [768], P('fsdp')
- grad_w_in: float32 [768, 768], P('fsdp')
- grad_in_bias: float32 [768], P('fsdp')
- grad_w_back: float32 [768, 768], P('fsdp')
- grad_back_bias: float32 [768], P('fsdp')
Inputs may be any that keep to these rules, and one draw needn't show every extreme that they name: `mol_len`: each slot of 256 tokens holds one molecule or is empty; the first slot of every device is used; on one device every slot is used and one slot is full, on another only the first is used.
All inputs are finite; a program needn't handle non-finite values.
Results may differ from a plain program's by a relative error of at most 0.012.
Values may be sent and summed in bfloat16 or wider, within the bound.
A program may use at most 192 MiB of HBM per device.

v0:
```python
import jax
import jax.numpy as jnp
from jax import lax
from jax.sharding import PartitionSpec as P

HEADS = 32


eps = 1e-05
masked_score = -1e30
group_heads = 8


def layer_norm(values, norm_gain, norm_shift):
    row_mean = jnp.mean(values, axis=-1, keepdims=True)
    centred = values - row_mean
    spread = jnp.mean(centred * centred, axis=-1, keepdims=True)
    return centred * lax.rsqrt(spread + eps) * norm_gain + norm_shift


def gelu_exact(values):
    return jax.nn.gelu(values, approximate=False)


def contract_rows(left, right):
    return jnp.einsum("rf,rd->fd", left, right, preferred_element_type=jnp.float32)


def against(left, right):
    return jnp.einsum("rd,fd->rf", left, right, preferred_element_type=jnp.float32)


def column_sums(values):
    return jnp.sum(values.astype(jnp.float32), axis=0)


def split_heads(values, block_count):
    total_rows, model_width = values.shape
    group_count = HEADS // group_heads
    head_dim = model_width // HEADS
    shaped = values.reshape(
        block_count, total_rows // block_count, group_count, group_heads, head_dim
    )
    return shaped.transpose(2, 0, 1, 3, 4)


def join_heads(values):
    group_count, block_count, block_rows, heads_here, head_dim = values.shape
    return values.transpose(1, 2, 0, 3, 4).reshape(
        block_count * block_rows, group_count * heads_here * head_dim
    )


def head_scores(queries, keys_here, allowed, score_scale):
    scores = (
        jnp.einsum("bqhd,bkhd->bhqk", queries, keys_here, preferred_element_type=jnp.float32)
        * score_scale
    )
    return jnp.where(allowed, scores, masked_score)


def per_device(
    tokens,
    mol_len,
    cotangent,
    ln1_gain,
    ln1_bias,
    w_qkv,
    q_bias,
    v_bias,
    w_out,
    out_bias,
    ln2_gain,
    ln2_bias,
    w_in,
    in_bias,
    w_back,
    back_bias,
):
    gathered = (
        lax.all_gather(ln1_gain, "fsdp", axis=0, tiled=True),
        lax.all_gather(ln1_bias, "fsdp", axis=0, tiled=True),
        lax.all_gather(w_qkv, "fsdp", axis=0, tiled=True),
        lax.all_gather(q_bias, "fsdp", axis=0, tiled=True),
        lax.all_gather(v_bias, "fsdp", axis=0, tiled=True),
        lax.all_gather(w_out, "fsdp", axis=0, tiled=True),
        lax.all_gather(out_bias, "fsdp", axis=0, tiled=True),
        lax.all_gather(ln2_gain, "fsdp", axis=0, tiled=True),
        lax.all_gather(ln2_bias, "fsdp", axis=0, tiled=True),
        lax.all_gather(w_in, "fsdp", axis=0, tiled=True),
        lax.all_gather(in_bias, "fsdp", axis=0, tiled=True),
        lax.all_gather(w_back, "fsdp", axis=0, tiled=True),
        lax.all_gather(back_bias, "fsdp", axis=0, tiled=True),
    )
    (
        gain_one,
        bias_one,
        full_qkv,
        full_qbias,
        full_vbias,
        full_out,
        full_obias,
        gain_two,
        bias_two,
        full_in,
        full_ibias,
        full_back,
        full_bbias,
    ) = gathered
    row_count, model_width = tokens.shape
    block_count = mol_len.shape[0]
    block_size = row_count // block_count
    score_scale = (model_width // HEADS) ** (-0.5)
    live_keys = jnp.arange(block_size)[None, :] < mol_len[:, None]
    row_valid = live_keys.reshape(row_count).astype(jnp.float32)[:, None]
    allowed = live_keys[:, None, None, :]

    def group_forward(pieces):
        q_group, k_group, v_group = pieces
        masked = head_scores(q_group, k_group, allowed, score_scale)
        row_peak = jnp.max(masked, axis=-1, keepdims=True)
        weights = jnp.exp(masked - row_peak)
        row_total = jnp.sum(weights, axis=-1, keepdims=True)
        soft_probs = (weights / row_total).astype(jnp.bfloat16)
        context = jnp.einsum(
            "bhqk,bkhd->bqhd", soft_probs, v_group, preferred_element_type=jnp.float32
        )
        return (context, row_peak, row_total)

    def group_backward(pieces):
        q_group, k_group, v_group, d_group, row_peak, row_total = pieces
        masked = head_scores(q_group, k_group, allowed, score_scale)
        soft_probs = jnp.exp(masked - row_peak) / row_total
        d_probs = jnp.einsum(
            "bqhd,bkhd->bhqk", d_group, v_group, preferred_element_type=jnp.float32
        )
        inner = jnp.sum(soft_probs * d_probs, axis=-1, keepdims=True)
        d_scores = jnp.where(allowed, soft_probs * (d_probs - inner), 0.0).astype(jnp.bfloat16)
        d_query = (
            jnp.einsum("bhqk,bkhd->bqhd", d_scores, k_group, preferred_element_type=jnp.float32)
            * score_scale
        )
        d_keys = (
            jnp.einsum("bhqk,bqhd->bkhd", d_scores, q_group, preferred_element_type=jnp.float32)
            * score_scale
        )
        d_values = jnp.einsum(
            "bhqk,bqhd->bkhd",
            soft_probs.astype(jnp.bfloat16),
            d_group,
            preferred_element_type=jnp.float32,
        )
        return (d_query, d_keys, d_values)

    inputs = tokens.astype(jnp.float32)
    normed_one, pull_one = jax.vjp(
        layer_norm, inputs, gain_one.astype(jnp.float32), bias_one.astype(jnp.float32)
    )
    normed_one_low = normed_one.astype(jnp.bfloat16)
    qkv_full = jnp.dot(normed_one_low, full_qkv, preferred_element_type=jnp.float32)
    query_low = (qkv_full[:, :model_width] + full_qbias.astype(jnp.float32)).astype(jnp.bfloat16)
    key_low = qkv_full[:, model_width : 2 * model_width].astype(jnp.bfloat16)
    value_low = (qkv_full[:, 2 * model_width :] + full_vbias.astype(jnp.float32)).astype(
        jnp.bfloat16
    )
    q_heads = split_heads(query_low, block_count)
    k_heads = split_heads(key_low, block_count)
    v_heads = split_heads(value_low, block_count)
    context, peak_all, total_all = lax.map(group_forward, (q_heads, k_heads, v_heads))
    context_low = join_heads(context).astype(jnp.bfloat16)
    attn_out = jnp.dot(
        context_low, full_out, preferred_element_type=jnp.float32
    ) + full_obias.astype(jnp.float32)
    mixed = inputs + row_valid * attn_out
    normed_two, pull_two = jax.vjp(
        layer_norm, mixed, gain_two.astype(jnp.float32), bias_two.astype(jnp.float32)
    )
    normed_two_low = normed_two.astype(jnp.bfloat16)
    pre_act = jnp.dot(
        normed_two_low, full_in, preferred_element_type=jnp.float32
    ) + full_ibias.astype(jnp.float32)
    activation, pull_act = jax.vjp(gelu_exact, pre_act)
    act_low = activation.astype(jnp.bfloat16)
    branch = jnp.dot(act_low, full_back, preferred_element_type=jnp.float32) + full_bbias.astype(
        jnp.float32
    )
    mixed_out = (mixed + row_valid * branch).astype(jnp.bfloat16)
    regathered = (
        lax.all_gather(w_qkv, "fsdp", axis=0, tiled=True),
        lax.all_gather(w_out, "fsdp", axis=0, tiled=True),
        lax.all_gather(w_in, "fsdp", axis=0, tiled=True),
        lax.all_gather(w_back, "fsdp", axis=0, tiled=True),
    )
    back_qkv, back_out, back_in, back_down = regathered
    upstream = cotangent.astype(jnp.float32)
    d_ffn = (row_valid * upstream).astype(jnp.bfloat16)
    grad_back = contract_rows(act_low, d_ffn)
    grad_bbias = column_sums(d_ffn)
    d_act = against(d_ffn, back_down)
    (d_pre,) = pull_act(d_act)
    d_pre_low = d_pre.astype(jnp.bfloat16)
    grad_in = contract_rows(normed_two_low, d_pre_low)
    grad_ibias = column_sums(d_pre_low)
    d_normed_two = against(d_pre_low, back_in)
    d_mixed_norm, grad_gain_two, grad_bias_two = pull_two(d_normed_two)
    d_mixed = upstream + d_mixed_norm
    d_attn = (row_valid * d_mixed).astype(jnp.bfloat16)
    grad_out = contract_rows(context_low, d_attn)
    grad_obias = column_sums(d_attn)
    d_context = against(d_attn, back_out).astype(jnp.bfloat16)
    d_heads = split_heads(d_context, block_count)
    d_query, d_keys, d_values = lax.map(
        group_backward, (q_heads, k_heads, v_heads, d_heads, peak_all, total_all)
    )
    d_query_low = join_heads(d_query).astype(jnp.bfloat16)
    d_keys_low = join_heads(d_keys).astype(jnp.bfloat16)
    d_values_low = join_heads(d_values).astype(jnp.bfloat16)
    d_qkv = jnp.concatenate([d_query_low, d_keys_low, d_values_low], axis=1)
    grad_qkv = contract_rows(normed_one_low, d_qkv)
    grad_qbias = column_sums(d_query_low)
    grad_vbias = column_sums(d_values_low)
    d_normed_one = against(d_qkv, back_qkv)
    d_inputs_norm, grad_gain_one, grad_bias_one = pull_one(d_normed_one)
    token_grad = (d_mixed + d_inputs_norm).astype(jnp.bfloat16)
    summed = (
        lax.psum_scatter(grad_gain_one, "fsdp", scatter_dimension=0, tiled=True),
        lax.psum_scatter(grad_bias_one, "fsdp", scatter_dimension=0, tiled=True),
        lax.psum_scatter(grad_qkv, "fsdp", scatter_dimension=0, tiled=True),
        lax.psum_scatter(grad_qbias, "fsdp", scatter_dimension=0, tiled=True),
        lax.psum_scatter(grad_vbias, "fsdp", scatter_dimension=0, tiled=True),
        lax.psum_scatter(grad_out, "fsdp", scatter_dimension=0, tiled=True),
        lax.psum_scatter(grad_obias, "fsdp", scatter_dimension=0, tiled=True),
        lax.psum_scatter(grad_gain_two, "fsdp", scatter_dimension=0, tiled=True),
        lax.psum_scatter(grad_bias_two, "fsdp", scatter_dimension=0, tiled=True),
        lax.psum_scatter(grad_in, "fsdp", scatter_dimension=0, tiled=True),
        lax.psum_scatter(grad_ibias, "fsdp", scatter_dimension=0, tiled=True),
        lax.psum_scatter(grad_back, "fsdp", scatter_dimension=0, tiled=True),
        lax.psum_scatter(grad_bbias, "fsdp", scatter_dimension=0, tiled=True),
    )
    return (
        mixed_out,
        token_grad,
        summed[0],
        summed[1],
        summed[2],
        summed[3],
        summed[4],
        summed[5],
        summed[6],
        summed[7],
        summed[8],
        summed[9],
        summed[10],
        summed[11],
        summed[12],
    )


def solution(mesh):
    placed = (
        P("fsdp", None),
        P("fsdp"),
        P("fsdp", None),
        P("fsdp"),
        P("fsdp"),
        P("fsdp", None),
        P("fsdp"),
        P("fsdp"),
        P("fsdp", None),
        P("fsdp"),
        P("fsdp"),
        P("fsdp"),
        P("fsdp", None),
        P("fsdp"),
        P("fsdp", None),
        P("fsdp"),
    )
    return jax.shard_map(
        per_device,
        mesh=mesh,
        in_specs=placed,
        out_specs=(
            P("fsdp", None),
            P("fsdp", None),
            P("fsdp"),
            P("fsdp"),
            P("fsdp", None),
            P("fsdp"),
            P("fsdp"),
            P("fsdp", None),
            P("fsdp"),
            P("fsdp"),
            P("fsdp"),
            P("fsdp", None),
            P("fsdp"),
            P("fsdp", None),
            P("fsdp"),
        ),
        check_vma=False,
    )
```

profile of v0, /device:TPU:0, one launch (start us, length us, event | category | flops | bytes accessed | tf_op | source)
XLA Modules:
  0.0 755.5 jit_solution(802317797004024377)
XLA Ops:
  17.6 42.6 %all-reduce.19 = (bf16[768]{0:T(1024)(128)(2,1)S(1)}, bf16[768]{0:T(1024)(128)(2,1)S(1)}, bf16[768]{0:T(1024)(128)(2,1)S(1)}, bf16[768]{0:T(1024)(128)(2,1)S(1)}...) all-reduce(bf16[768]{0:T(1024)(128)(2,1)S(1)} %dynamic-update-slice, ...), channel_id=1, replica_groups=mesh['fsdp'=32] {'fsdp'}, use_global_device_ids=true, to_apply=%add.1 | all-reduce | flops 6912 | bytes 27648
  68.6 4.7 copy.89
  73.8 10.0 %fusion.86 = f32[2048,2304]{1,0:T(8,128)S(1)} fusion(bf16[768,2304]{1,0:T(8,128)(2,1)} %all-gather.5.cloned.1.call-done, bf16[2048,768]{0,1:T(8,128)(2,1)S(1)} %copy.80, f32[768]{0:T(1024)S(1)} %convert_element_type.149, f32[768]{0:T(1024)S(1)} %convert_element_type.148, f32[2048]{0:T(1024)S(1)} %fusion.82, f32[2048]{0:T(1024)S(1)} %broadcast_multiply_fusion.1), kind=kOutput, calls=%fused_computation.136 | convolution fusion | flops 7257194496 | bytes 25581568 | tf_op jit(solution)/shard_map/dot_general | solution.py:160
  94.3 4.6 copy.83
  104.3 4.6 copy.81
  116.4 66.1 %while.30 = (s32[]{:T(128)}, bf16[4,8,256,8,24]{2,4,3,1,0:T(8,128)(2,1)}, f32[4,8,8,256,1]{3,2,1,4,0:T(8,128)}, f32[4,8,8,256,1]{3,2,1,4,0:T(8,128)S(1)}, bf16[4...) while((s32[]{:T(128)}, ...), condition=%wide.region_5.6_spmd.clone, body=%wide.region_2.5_spmd.clone.sunk | while | flops 452954112 | bytes 80029888 | solution.py:169
  116.4 5.4 fusion.131
  121.8 4.1 fusion.132
  126.0 5.1 bitcast_dynamic-update-slice_fusion.11
  132.9 5.3 fusion.131
  138.3 4.1 fusion.132
  142.4 5.1 bitcast_dynamic-update-slice_fusion.11
  149.3 5.4 fusion.131
  154.7 4.1 fusion.132
  158.9 5.1 bitcast_dynamic-update-slice_fusion.11
  165.8 5.4 fusion.131
  171.1 4.1 fusion.132
  175.3 5.1 bitcast_dynamic-update-slice_fusion.11
  184.2 4.6 copy.87
  191.6 5.7 fusion.90
  202.6 19.6 %multiply_convert_fusion.1 = (bf16[2048,768]{1,0:T(8,128)(2,1)}, f32[2048,768]{1,0:T(8,128)}, f32[2048,768]{1,0:T(8,128)}) fusion(f32[768]{0:T(1024)S(1)} %copy-done.42, bf16[2048,768]{0,1:T(8,128)(2,1)} %add_convert_fusion.3, bf16[768,768]{1,0:T(8,128)(2,1)} %all-gather.9.cloned.1.call-done), kind=kOutput, calls=%fused_computation.96 | convolution fusion | flops 2519728128 | bytes 20057088 | tf_op jit(solution)/shard_map/dot_general | solution.py:179
  222.2 19.2 %all-gather.11.cloned.1.call-done = bf16[768,768]{1,0:T(8,128)(2,1)} async-done(((bf16[24,768]{1,0:T(8,128)(2,1)}), bf16[768,768]{1,0:T(8,128)(2,1)}) %all-gather.11.cloned.1.call-update) | async-done | bytes 1179664 | tf_op jit(solution)/shard_map/all_gather | solution.py:92
  241.4 8.9 %convert_reduce_fusion.2 = (f32[768]{0:T(1024)}, bf16[2048,768]{1,0:T(8,128)(2,1)S(1)}) fusion(f32[2048,768]{1,0:T(8,128)} %get-tuple-element.316, bf16[768,768]{1,0:T(8,128)(2,1)} %all-gather.11.cloned.1.call-done, bf16[2048,768]{0,1:T(8,128)(2,1)S(1)} %copy-done.11, f32[2048]{0:T(1024)S(1)} %bitcast.198, f32[2048,768]{1,0:T(8,128)} %get-tuple-element.328, ...), kind=kOutput, calls=%fused_computation.86 | convolution fusion | flops 2447375616 | bytes 20068352 | tf_op jit(solution)/shard_map/rd,fd->rf/dot_general | solution.py:30
  252.0 4.1 fusion.94
  256.1 8.1 %fusion.92 = (f32[768]{0:T(1024)}, f32[2048,768]{1,0:T(8,128)}) fusion(bf16[2048,768]{1,0:T(8,128)(2,1)} %copy-done.46, bf16[768,768]{1,0:T(8,128)(2,1)} %all-gather.9.cloned.1.call-done), kind=kOutput, calls=%fused_computation.140 | convolution fusion | flops 2417491200 | bytes 10619904 | tf_op jit(solution)/shard_map/rd,fd->rf/dot_general | solution.py:30
  264.3 6.9 copy.90
  271.2 6.0 fusion.75
  277.2 6.4 multiply_reduce_fusion.1
  283.6 5.8 fusion.88
  294.1 4.1 convolution_convert_fusion
  305.4 4.1 fusion.93
  315.7 285.0 %while.31 = (s32[]{:T(128)}, bf16[4,8,256,8,24]{2,4,3,1,0:T(8,128)(2,1)}, bf16[4,8,256,8,24]{2,4,3,1,0:T(8,128)(2,1)}, bf16[4,8,256,8,24]{2,4,3,1,0:T(8,128)(2,1...) while((s32[]{:T(128)}, ...), condition=%wide.region_12.13_spmd.clone, body=%wide.region_10.12_spmd.clone.sunk | while | flops 1070369280 | bytes 289025248 | solution.py:212
  318.2 6.5 exponential_divide_fusion.2
  324.7 3.9 bitcast_dynamic-update-slice_fusion.15
  330.6 9.2 %fusion.142 = f32[8,8,256,256]{2,3,1,0:T(8,128)} fusion(bf16[4,8,256,8,24]{2,4,3,1,0:T(8,128)(2,1)} %get-tuple-element.525, s32[]{:T(128)S(6)} %copy.157, bf16[1,8,256,8,24]{2,1,4,3,0:T(8,128)(2,1)S(1)} %constant_dynamic-slice_fusion.2), kind=kOutput, calls=%fused_computation.37.clone.1 | convolution fusion | flops 201326592 | bytes 18350084 | tf_op jit(solution)/shard_map/while/body/eval_jaxpr/bqhd,bkhd->bhqk/dot_general | solution.py:134
  339.9 23.2 %bitcast_dynamic-update-slice_fusion.14 = bf16[4,8,256,8,24]{2,4,3,1,0:T(8,128)(2,1)} fusion(bf16[4,8,256,8,24]{2,4,3,1,0:T(8,128)(2,1)} %get-tuple-element.506, s32[]{:T(128)S(6)} %copy.157, f32[8,8,256,256]{2,3,1,0:T(8,128)} %copy-done, f32[8,8,256,256]{2,3,1,0:T(8,128)} %fusion.142, pred[8,256]{1,0:T(8,128)(4,1)S(1)} %fusion.141, ...), kind=kOutput, calls=%fused_computation.34.clone.1 | convolution fusion | flops 222707968 | bytes 69471232 | tf_op jit(solution)/shard_map/while/body/eval_jaxpr/bhqk,bqhd->bkhd/dot_general | solution.py:144
  363.1 22.5 %bitcast_dynamic-update-slice_fusion.13 = bf16[4,8,256,8,24]{2,4,3,1,0:T(8,128)(2,1)S(1)} fusion(bf16[4,8,256,8,24]{2,4,3,1,0:T(8,128)(2,1)S(1)} %copy-done.8, s32[]{:T(128)S(6)} %copy.157, f32[8,8,256,256]{2,3,1,0:T(8,128)} %copy-done, f32[8,8,256,256]{2,3,1,0:T(8,128)} %fusion.142, pred[8,256]{1,0:T(8,128)(4,1)S(1)} %fusion.141, ...), kind=kOutput, calls=%fused_computation.35.clone.1 | convolution fusion | flops 222707968 | bytes 69471232 | tf_op jit(solution)/shard_map/while/body/eval_jaxpr/bhqk,bkhd->bqhd/dot_general | solution.py:140
  389.4 6.5 exponential_divide_fusion.2
  395.9 3.9 bitcast_dynamic-update-slice_fusion.15
  401.9 9.4 %fusion.142 = f32[8,8,256,256]{2,3,1,0:T(8,128)} fusion(bf16[4,8,256,8,24]{2,4,3,1,0:T(8,128)(2,1)} %get-tuple-element.525, s32[]{:T(128)S(6)} %copy.157, bf16[1,8,256,8,24]{2,1,4,3,0:T(8,128)(2,1)S(1)} %constant_dynamic-slice_fusion.2), kind=kOutput, calls=%fused_computation.37.clone.1 | convolution fusion | flops 201326592 | bytes 18350084 | tf_op jit(solution)/shard_map/while/body/eval_jaxpr/bqhd,bkhd->bhqk/dot_general | solution.py:134
  411.3 23.4 %bitcast_dynamic-update-slice_fusion.14 = bf16[4,8,256,8,24]{2,4,3,1,0:T(8,128)(2,1)} fusion(bf16[4,8,256,8,24]{2,4,3,1,0:T(8,128)(2,1)} %get-tuple-element.506, s32[]{:T(128)S(6)} %copy.157, f32[8,8,256,256]{2,3,1,0:T(8,128)} %copy-done, f32[8,8,256,256]{2,3,1,0:T(8,128)} %fusion.142, pred[8,256]{1,0:T(8,128)(4,1)S(1)} %fusion.141, ...), kind=kOutput, calls=%fused_computation.34.clone.1 | convolution fusion | flops 222707968 | bytes 69471232 | tf_op jit(solution)/shard_map/while/body/eval_jaxpr/bhqk,bqhd->bkhd/dot_general | solution.py:144
  434.7 22.0 %bitcast_dynamic-update-slice_fusion.13 = bf16[4,8,256,8,24]{2,4,3,1,0:T(8,128)(2,1)S(1)} fusion(bf16[4,8,256,8,24]{2,4,3,1,0:T(8,128)(2,1)S(1)} %copy-done.8, s32[]{:T(128)S(6)} %copy.157, f32[8,8,256,256]{2,3,1,0:T(8,128)} %copy-done, f32[8,8,256,256]{2,3,1,0:T(8,128)} %fusion.142, pred[8,256]{1,0:T(8,128)(4,1)S(1)} %fusion.141, ...), kind=kOutput, calls=%fused_computation.35.clone.1 | convolution fusion | flops 222707968 | bytes 69471232 | tf_op jit(solution)/shard_map/while/body/eval_jaxpr/bhqk,bkhd->bqhd/dot_general | solution.py:140
  460.5 6.5 exponential_divide_fusion.2
  467.0 3.9 bitcast_dynamic-update-slice_fusion.15
  472.9 9.3 %fusion.142 = f32[8,8,256,256]{2,3,1,0:T(8,128)} fusion(bf16[4,8,256,8,24]{2,4,3,1,0:T(8,128)(2,1)} %get-tuple-element.525, s32[]{:T(128)S(6)} %copy.157, bf16[1,8,256,8,24]{2,1,4,3,0:T(8,128)(2,1)S(1)} %constant_dynamic-slice_fusion.2), kind=kOutput, calls=%fused_computation.37.clone.1 | convolution fusion | flops 201326592 | bytes 18350084 | tf_op jit(solution)/shard_map/while/body/eval_jaxpr/bqhd,bkhd->bhqk/dot_general | solution.py:134
  482.3 23.8 %bitcast_dynamic-update-slice_fusion.14 = bf16[4,8,256,8,24]{2,4,3,1,0:T(8,128)(2,1)} fusion(bf16[4,8,256,8,24]{2,4,3,1,0:T(8,128)(2,1)} %get-tuple-element.506, s32[]{:T(128)S(6)} %copy.157, f32[8,8,256,256]{2,3,1,0:T(8,128)} %copy-done, f32[8,8,256,256]{2,3,1,0:T(8,128)} %fusion.142, pred[8,256]{1,0:T(8,128)(4,1)S(1)} %fusion.141, ...), kind=kOutput, calls=%fused_computation.34.clone.1 | convolution fusion | flops 222707968 | bytes 69471232 | tf_op jit(solution)/shard_map/while/body/eval_jaxpr/bhqk,bqhd->bkhd/dot_general | solution.py:144
  506.1 22.3 %bitcast_dynamic-update-slice_fusion.13 = bf16[4,8,256,8,24]{2,4,3,1,0:T(8,128)(2,1)S(1)} fusion(bf16[4,8,256,8,24]{2,4,3,1,0:T(8,128)(2,1)S(1)} %copy-done.8, s32[]{:T(128)S(6)} %copy.157, f32[8,8,256,256]{2,3,1,0:T(8,128)} %copy-done, f32[8,8,256,256]{2,3,1,0:T(8,128)} %fusion.142, pred[8,256]{1,0:T(8,128)(4,1)S(1)} %fusion.141, ...), kind=kOutput, calls=%fused_computation.35.clone.1 | convolution fusion | flops 222707968 | bytes 69471232 | tf_op jit(solution)/shard_map/while/body/eval_jaxpr/bhqk,bkhd->bqhd/dot_general | solution.py:140
  532.2 6.5 exponential_divide_fusion.2
  538.7 4.0 bitcast_dynamic-update-slice_fusion.15
  544.7 9.2 %fusion.142 = f32[8,8,256,256]{2,3,1,0:T(8,128)} fusion(bf16[4,8,256,8,24]{2,4,3,1,0:T(8,128)(2,1)} %get-tuple-element.525, s32[]{:T(128)S(6)} %copy.157, bf16[1,8,256,8,24]{2,1,4,3,0:T(8,128)(2,1)S(1)} %constant_dynamic-slice_fusion.2), kind=kOutput, calls=%fused_computation.37.clone.1 | convolution fusion | flops 201326592 | bytes 18350084 | tf_op jit(solution)/shard_map/while/body/eval_jaxpr/bqhd,bkhd->bhqk/dot_general | solution.py:134
  553.9 23.1 %bitcast_dynamic-update-slice_fusion.14 = bf16[4,8,256,8,24]{2,4,3,1,0:T(8,128)(2,1)} fusion(bf16[4,8,256,8,24]{2,4,3,1,0:T(8,128)(2,1)} %get-tuple-element.506, s32[]{:T(128)S(6)} %copy.157, f32[8,8,256,256]{2,3,1,0:T(8,128)} %copy-done, f32[8,8,256,256]{2,3,1,0:T(8,128)} %fusion.142, pred[8,256]{1,0:T(8,128)(4,1)S(1)} %fusion.141, ...), kind=kOutput, calls=%fused_computation.34.clone.1 | convolution fusion | flops 222707968 | bytes 69471232 | tf_op jit(solution)/shard_map/while/body/eval_jaxpr/bhqk,bqhd->bkhd/dot_general | solution.py:144
  577.1 21.8 %bitcast_dynamic-update-slice_fusion.13 = bf16[4,8,256,8,24]{2,4,3,1,0:T(8,128)(2,1)S(1)} fusion(bf16[4,8,256,8,24]{2,4,3,1,0:T(8,128)(2,1)S(1)} %copy-done.8, s32[]{:T(128)S(6)} %copy.157, f32[8,8,256,256]{2,3,1,0:T(8,128)} %copy-done, f32[8,8,256,256]{2,3,1,0:T(8,128)} %fusion.142, pred[8,256]{1,0:T(8,128)(4,1)S(1)} %fusion.141, ...), kind=kOutput, calls=%fused_computation.35.clone.1 | convolution fusion | flops 222707968 | bytes 69471232 | tf_op jit(solution)/shard_map/while/body/eval_jaxpr/bhqk,bkhd->bqhd/dot_general | solution.py:140
  600.7 4.6 copy.97
  618.9 10.1 %fusion.84 = f32[768,2304]{1,0:T(8,128)} fusion(bf16[2048,2304]{0,1:T(8,128)(2,1)S(1)} %constant_dynamic-update-slice_fusion, bf16[2048,768]{0,1:T(8,128)(2,1)S(1)} %copy-done.3, f32[768]{0:T(1024)S(1)} %copy-done.41, f32[768]{0:T(1024)S(1)} %copy-done.29, f32[2048]{0:T(1024)S(1)} %copy-done.25, f32[2048]{0:T(1024)S(1)} %copy-done.21), kind=kOutput, calls=%fused_computation.135 | convolution fusion | flops 7257194496 | bytes 19683328 | tf_op jit(solution)/shard_map/rf,rd->fd/dot_general | solution.py:26
  629.6 8.7 %add_convert_fusion.2 = bf16[2048,768]{0,1:T(8,128)(2,1)} fusion(f32[2048,768]{0,1:T(8,128)} %copy-done.4, bf16[2048,768]{1,0:T(8,128)(2,1)} %get-tuple-element.315, bf16[768,768]{1,0:T(8,128)(2,1)} %all-gather.11.cloned.1.call-done, f32[768]{0:T(1024)S(1)} %convert_element_type.164, f32[2048]{0:T(1024)S(1)} %bitcast.201), kind=kOutput, calls=%fused_computation.95 | convolution fusion | flops 2422210560 | bytes 13773824 | tf_op jit(solution)/shard_map/dot_general | solution.py:184
  638.3 4.7 copy.102
  643.0 3.9 convert_reduce_fusion.4
  647.1 13.2 %fusion.91 = (f32[768]{0:T(1024)S(1)}, f32[2048,768]{1,0:T(8,128)}) fusion(bf16[2048,2304]{0,1:T(8,128)(2,1)} %copy-done.19, bf16[768,2304]{1,0:T(8,128)(2,1)} %all-gather.5.cloned.1.call-done), kind=kOutput, calls=%fused_computation.139 | convolution fusion | flops 7249329152 | bytes 19270656 | tf_op jit(solution)/shard_map/rd,fd->rf/dot_general | solution.py:30
  660.3 7.0 copy.99
  667.4 4.1 fusion.66
  675.4 41.2 %all-reduce.18 = (f32[768]{0:T(1024)S(1)}, f32[768]{0:T(1024)S(1)}, f32[768]{0:T(1024)S(1)}, f32[768]{0:T(1024)S(1)}, f32[768]{0:T(1024)S(1)}, /*index=5*/f32[76...) all-reduce(f32[768]{0:T(1024)S(1)} %get-tuple-element.253, ...), channel_id=2, replica_groups=mesh['fsdp'=32] {'fsdp'}, use_global_device_ids=true, to_apply=%region_16.17.clone | all-reduce | flops 6912 | bytes 55296
  721.8 8.4 %add_convert_fusion = bf16[2048,768]{0,1:T(8,128)(2,1)} fusion(f32[2048,768]{0,1:T(8,128)} %copy-done.6, bf16[2048,768]{0,1:T(8,128)(2,1)} %copy.89, f32[2048]{0:T(1024)S(1)} %negate_multiply_fusion.1, f32[2048]{0:T(1024)S(1)} %copy-done.27, f32[2048]{0:T(1024)S(1)} %multiply_multiply_fusion.5, f32[2048]{0:T(1024)S(1)} %copy-done.21, ...), kind=kLoop, calls=%fused_computation.91 | loop fusion | flops 20447232 | bytes 22064128 | tf_op jit(solution)/shard_map/convert_element_type | solution.py:224
  730.2 4.6 copy.103
  734.8 13.3 %reduce-scatter.5.cloned.1.call-done = f32[24,2304]{1,0:T(8,128)} async-done(((f32[768,2304]{1,0:T(8,128)}), f32[24,2304]{1,0:T(8,128)}) %reduce-scatter.5.cloned.1.call-update) | async-done | bytes 221200 | tf_op jit(solution)/shard_map/reduce_scatter | solution.py:228
  (247 shorter events, 125.4 us)
Async XLA Ops:
  7.2 66.7 %all-gather.5.cloned.1.call-start = ((), (), s32[]{:S(2)}) async-start(), calls=%async_computation.4 | async-start | bytes 3649536 | tf_op jit(solution)/shard_map/all_gather | solution.py:83
  7.9 183.7 %all-gather.7.cloned.1.call-start = ((), (), s32[]{:S(2)}) async-start(), calls=%async_computation.5 | async-start | bytes 1216512 | tf_op jit(solution)/shard_map/all_gather | solution.py:86
  8.7 193.9 %all-gather.9.cloned.1.call-start = ((), (), s32[]{:S(2)}) async-start(), calls=%async_computation.6 | async-start | bytes 1216512 | tf_op jit(solution)/shard_map/all_gather | solution.py:90
  9.4 232.0 %all-gather.11.cloned.1.call-start = ((), (), s32[]{:S(2)}) async-start(), calls=%async_computation.7 | async-start | bytes 1216512 | tf_op jit(solution)/shard_map/all_gather | solution.py:92
  10.0 724.9 %reduce-scatter.9.cloned.1.call-start = ((), (), s32[]{:S(2)}) async-start(), calls=%async_computation.10 | async-start | bytes 2433024 | tf_op jit(solution)/shard_map/reduce_scatter | solution.py:235
  60.2 13.7 %copy-start.40 = (f32[768]{0:T(1024)}, f32[768]{0:T(1024)S(1)}, u32[]{:S(2)}) copy-start(f32[768]{0:T(1024)S(1)} %convert_element_type.149) | copy-start | bytes 9220
  60.2 13.7 %copy-start.28 = (f32[768]{0:T(1024)}, f32[768]{0:T(1024)S(1)}, u32[]{:S(2)}) copy-start(f32[768]{0:T(1024)S(1)} %convert_element_type.148) | copy-start | bytes 9220
  67.1 6.7 copy-start.1
  67.7 16.2 %copy-start.20 = (f32[2048]{0:T(1024)}, f32[2048]{0:T(1024)S(1)}, u32[]{:S(2)}) copy-start(f32[2048]{0:T(1024)S(1)} %broadcast_multiply_fusion.1) | copy-start | bytes 24580
  68.5 15.4 %copy-start.22 = (f32[2048]{0:T(1024)}, f32[2048]{0:T(1024)S(1)}, u32[]{:S(2)}) copy-start(f32[2048]{0:T(1024)S(1)} %fusion.65) | copy-start | bytes 24580
  68.5 15.4 %copy-start.24 = (f32[2048]{0:T(1024)}, f32[2048]{0:T(1024)S(1)}, u32[]{:S(2)}) copy-start(f32[2048]{0:T(1024)S(1)} %fusion.82) | copy-start | bytes 24580
  111.9 4.5 copy-start.31
  121.8 4.2 copy-start.13
  131.1 1.7 copy-start.14
  138.3 4.2 copy-start.13
  147.6 1.7 copy-start.14
  154.7 4.2 copy-start.13
  164.0 1.7 copy-start.14
  171.1 4.2 copy-start.13
  180.4 1.7 copy-start.14
  182.5 1.7 copy-start.12
  184.2 7.4 copy-start.2
  184.2 7.4 copy-start.32
  184.2 7.4 copy-start.43
  197.3 2.6 copy-start.4
  197.3 2.6 copy-start.30
  197.3 2.6 copy-start.37
  198.0 4.5 copy-start.42
  202.6 38.9 %copy-start.11 = (bf16[2048,768]{0,1:T(8,128)(2,1)S(1)}, bf16[2048,768]{0,1:T(8,128)(2,1)}, u32[]{:S(2)}) copy-start(bf16[2048,768]{0,1:T(8,128)(2,1)} %copy.89) | copy-start | bytes 9437188
  241.4 10.6 %copy-start.16 = (bf16[2048,768]{0,1:T(8,128)(2,1)S(1)}, bf16[2048,768]{0,1:T(8,128)(2,1)}, u32[]{:S(2)}) copy-start(bf16[2048,768]{0,1:T(8,128)(2,1)} %add_convert_fusion.3) | copy-start | bytes 9437188
  256.1 478.8 %reduce-scatter.11.cloned.1.call-start = ((), (), s32[]{:S(2)}) async-start(), calls=%async_computation.11 | async-start | bytes 2433024 | tf_op jit(solution)/shard_map/reduce_scatter | solution.py:237
  277.2 457.7 %reduce-scatter.7.cloned.1.call-start = ((), (), s32[]{:S(2)}) async-start(), calls=%async_computation.9 | async-start | bytes 2433024 | tf_op jit(solution)/shard_map/reduce_scatter | solution.py:231
  289.4 3.0 copy-start.6
  289.4 3.0 copy-start.26
  289.5 4.6 copy-start.45
  301.4 2.8 copy-start.15
  301.4 4.1 copy-start.18
  309.6 438.6 %reduce-scatter.5.cloned.1.call-start = ((), (), s32[]{:S(2)}) async-start(), calls=%async_computation.8 | async-start | bytes 7299072 | tf_op jit(solution)/shard_map/reduce_scatter | solution.py:228
  324.7 6.0 copy-start
  339.9 23.2 %copy-start.8 = (bf16[4,8,256,8,24]{2,4,3,1,0:T(8,128)(2,1)S(1)}, bf16[4,8,256,8,24]{2,4,3,1,0:T(8,128)(2,1)}, u32[]{:S(2)}) copy-start(bf16[4,8,256,8,24]{2,4,3,1,0:T(8,128)(2,1)} %get-tuple-element.505) | copy-start | bytes 9437188 | tf_op jit(solution)/shard_map/while
  385.6 1.7 copy-start.9
  395.9 6.0 copy-start
  411.3 23.4 %copy-start.8 = (bf16[4,8,256,8,24]{2,4,3,1,0:T(8,128)(2,1)S(1)}, bf16[4,8,256,8,24]{2,4,3,1,0:T(8,128)(2,1)}, u32[]{:S(2)}) copy-start(bf16[4,8,256,8,24]{2,4,3,1,0:T(8,128)(2,1)} %get-tuple-element.505) | copy-start | bytes 9437188 | tf_op jit(solution)/shard_map/while
  456.7 1.7 copy-start.9
  467.0 6.0 copy-start
  482.3 23.8 %copy-start.8 = (bf16[4,8,256,8,24]{2,4,3,1,0:T(8,128)(2,1)S(1)}, bf16[4,8,256,8,24]{2,4,3,1,0:T(8,128)(2,1)}, u32[]{:S(2)}) copy-start(bf16[4,8,256,8,24]{2,4,3,1,0:T(8,128)(2,1)} %get-tuple-element.505) | copy-start | bytes 9437188 | tf_op jit(solution)/shard_map/while
  538.7 6.0 copy-start
  553.9 23.1 %copy-start.8 = (bf16[4,8,256,8,24]{2,4,3,1,0:T(8,128)(2,1)S(1)}, bf16[4,8,256,8,24]{2,4,3,1,0:T(8,128)(2,1)}, u32[]{:S(2)}) copy-start(bf16[4,8,256,8,24]{2,4,3,1,0:T(8,128)(2,1)} %get-tuple-element.505) | copy-start | bytes 9437188 | tf_op jit(solution)/shard_map/while
  600.7 5.7 copy-start.10
  606.4 3.7 copy-start.7
  614.2 4.7 copy-start.3
  614.2 4.7 copy-start.21
  614.2 4.7 copy-start.25
  614.2 4.6 copy-start.29
  614.2 4.6 copy-start.41
  615.2 3.6 copy-start.19
  667.3 4.2 copy-start.23
  667.4 4.8 copy-start.5
  671.5 3.8 copy-start.34
  671.5 3.8 copy-start.35
  671.5 3.8 copy-start.36
  671.5 3.8 copy-start.38
  671.6 3.8 copy-start.39
  671.6 50.2 %copy-start.27 = (f32[2048]{0:T(1024)S(1)}, f32[2048]{0:T(1024)}, u32[]{:S(2)}) copy-start(f32[2048]{0:T(1024)} %copy-done.26) | copy-start | bytes 24580
  (6 other events, 7.9 us)
Sparse Core Ops, SparseCore 0:
  10.9 62.8 all-gather.4
  76.7 52.9 all-gather.6
  132.7 52.9 all-gather.8
  188.4 52.9 all-gather.10
  256.2 97.9 reduce-scatter.8
  360.8 98.0 reduce-scatter.10
  464.7 97.9 reduce-scatter.6
  629.1 119.0 reduce-scatter.4
where the time goes:
time: 767 us; the launch traced here: 755 us
  matrix products  406 us (53%)
  local copies, waits for them, and re-layouts  150 us (20%)
  blocking collectives  83.8 us (11%)
  other arithmetic  63 us (8%)
  waiting for transfers between devices  35.8 us (5%)
  between operations  15.2 us (2%)
    dot_general x4, matrix products, group_backward(): jnp.einsum('bhqk,bqhd->bkhd', d_scores, q_group, preferred_element_type=j...  93.5 us
    dot_general x4, matrix products, group_backward(): jnp.einsum('bhqk,bkhd->bqhd', d_scores, k_group, preferred_element_type=j...  88.6 us
    unnamed x2, blocking collectives  83.8 us
    unnamed x129, local copies, waits for them, and re-layouts  66 us
    dot_general x8, matrix products, head_scores(): jnp.einsum('bqhd,bkhd->bhqk', queries, keys_here, preferred_element_type=...  47.4 us
    dot_general x4, matrix products, group_backward(): jnp.einsum('bqhd,bkhd->bhqk', d_group, v_group, preferred_element_type=jn...  37.2 us
    dot_general x4, matrix products, against(): jnp.einsum('rd,fd->rf', left, right, preferred_element_type=jnp.float32)  34.4 us
    dot_general x4, matrix products, contract_rows(): jnp.einsum('rf,rd->fd', left, right, preferred_element_type=jnp.float32)  24.2 us
  transfers between devices with their start and end apart: 8, of which 3 were waited for; matrix products, arithmetic and copies ran while one was open for 76% of the time, Pallas kernels for 0%

commit v1 on v0

v1 whole, which is shorter than its diff:
```python
import functools

import jax
import jax.numpy as jnp
from jax import lax
from jax.experimental import pallas as pl
from jax.experimental.pallas import tpu as pltpu
from jax.sharding import PartitionSpec as P

HEADS = 32

bf16 = jnp.bfloat16
f32 = jnp.float32
eps = 1e-05
masked_score = -1e30
log2_e = 1.4426950408889634
MESH = pl.DeviceIdType.MESH
MIB = 1 << 20

PLANES = 4
CHIPS = 4 * PLANES
DEVICES = 2 * CHIPS
SHARD = 24


def dot(left, right, left_dim, right_dim):
    return lax.dot_general(
        left, right, (((left_dim,), (right_dim,)), ((), ())), preferred_element_type=f32
    )


def normalize(values):
    centred = values - jnp.mean(values, axis=-1, keepdims=True)
    factor = lax.rsqrt(jnp.mean(centred * centred, axis=-1, keepdims=True) + eps)
    return centred * factor, factor


def norm_backward(d_normed, gain, unit, factor):
    e = d_normed * gain
    inner = jnp.mean(e * unit, axis=-1, keepdims=True)
    return factor * (e - jnp.mean(e, axis=-1, keepdims=True) - unit * inner)


def fold_rows(values):
    rows, columns = values.shape
    return jnp.sum(values.reshape(rows // 8, 8, columns), axis=0)


class Place:
    def __init__(self):
        me = lax.axis_index("fsdp")
        self.me = me
        self.c = lax.rem(me, 2)
        self.x = lax.rem(me // 2, 2)
        self.y = lax.rem(me // 4, 2)
        self.z = me // 8
        self.sib = me + 1 - 2 * self.c
        self.xn = me + 2 - 4 * self.x
        self.yn = me + 4 - 8 * self.y
        self.up = me + 8
        self.down = me - 8

    def block(self, c, z, y, x):
        return ((c * PLANES + z) * 2 + y) * 2 + x

    def barrier(self):
        sem = pltpu.get_barrier_semaphore()

        def greet(device):
            pl.semaphore_signal(sem, inc=1, device_id=(device,), device_id_type=MESH)

        for device in (self.sib, self.xn, self.yn):
            greet(device)

        @pl.when(self.z < PLANES - 1)
        def _():
            greet(self.up)

        @pl.when(self.z > 0)
        def _():
            greet(self.down)

        inner = jnp.where((self.z > 0) & (self.z < PLANES - 1), 5, 4)
        pl.semaphore_wait(sem, inner)


def gather_kernel(
    small_ref,
    wq_ref,
    wo_ref,
    wi_ref,
    wb_ref,
    tok_ref,
    qkv_hbm,
    unit_hbm,
    fq_hbm,
    fo_hbm,
    fi_hbm,
    fb_hbm,
    vec_ref,
    gq,
    goi,
    gb,
    fq,
    fo,
    fi,
    fb,
    fq_t,
    unit,
    unit_t,
    qkv,
    bias,
    send_sem,
    recv_sem,
    copy_sem,
):
    at = Place()
    width = tok_ref.shape[1]
    slots, _, block = qkv.shape
    slabs = (gq, goi, gb)
    half_q = 3 * width // 2
    half = width // 2
    own = at.block(at.c, at.z, at.y, at.x)

    gq[own] = jnp.concatenate(
        [
            jnp.concatenate([wq_ref[:, :half_q], wq_ref[:, half_q:]], axis=0),
            jnp.concatenate([small_ref[...], jnp.zeros((2 * SHARD - 16, 128), bf16)], axis=0),
        ],
        axis=1,
    )
    goi[own] = jnp.concatenate([wo_ref[...], wi_ref[...]], axis=0)
    gb[own] = jnp.concatenate([wb_ref[:, :half], wb_ref[:, half:]], axis=0)

    pending = []

    def remote(k, first, count, target, kind):
        view = slabs[k].at[pl.ds(first, count)]
        return pltpu.make_async_remote_copy(
            src_ref=view,
            dst_ref=view,
            send_sem=send_sem.at[k, lax.rem(first, CHIPS), kind],
            recv_sem=recv_sem.at[k, first],
            device_id=(target,),
            device_id_type=MESH,
        )

    def send(k, first, target, kind, count=1, when=None):
        copy = remote(k, first, count, target, kind)
        pending.append((copy, when))

        if when is None:
            copy.start()
        else:
            pl.when(when)(copy.start)

    def arrived(k, first, count=1):
        remote(k, first, count, at.sib, 0).wait_recv()

    below = at.z > 0
    above = at.z < PLANES - 1

    def own_sends(k):
        send(k, own, at.xn, 1)
        send(k, own, at.yn, 2)
        send(k, own, at.up, 3, when=above)
        send(k, own, at.down, 4, when=below)
        send(k, own, at.sib, 0)

    def column(k, s):
        lower = at.z - s >= 0
        upper = at.z + s <= PLANES - 1
        for there, shift, onward, target, kind in (
            (lower, -s, above, at.up, 3),
            (upper, s, below, at.down, 4),
        ):
            b = own + 4 * shift

            @pl.when(there)
            def _():
                arrived(k, b)

            send(k, b, target, kind, when=there & onward)
            send(k, b, at.xn, 1, when=there)
            send(k, b, at.yn, 2, when=there)
            send(k, b, at.sib, 0, when=there)

    def plane(k, s):
        for shift in sorted({-s, s}):
            level = at.z + shift
            there = (level >= 0) & (level <= PLANES - 1)
            even = lax.rem(level, 2) == 0
            for b, target, kind, onward in (
                (at.block(at.c, level, at.y, 1 - at.x), at.yn, 2, even),
                (at.block(at.c, level, 1 - at.y, at.x), at.xn, 1, jnp.logical_not(even)),
            ):

                @pl.when(there)
                def _():
                    arrived(k, b)

                send(k, b, target, kind, when=there & onward)
                send(k, b, at.sib, 0, when=there)

    def corner(k, j):
        b = at.block(at.c, j, 1 - at.y, 1 - at.x)
        arrived(k, b)
        send(k, b, at.sib, 0)

    def others(k):
        for j in range(PLANES):
            for i in range(4):
                arrived(k, (1 - at.c) * CHIPS + 4 * j + i)

    def flat(k):
        even = lax.rem(at.z, 2) == 0
        x_block = at.block(at.c, at.z, at.y, 1 - at.x)
        y_block = at.block(at.c, at.z, 1 - at.y, at.x)
        z_block = at.block(at.c, at.z, 1 - at.y, 1 - at.x)
        arrived(k, x_block)
        send(k, x_block, at.yn, 2, when=even)
        arrived(k, y_block)
        send(k, y_block, at.xn, 1, when=jnp.logical_not(even))
        for b in (x_block, y_block):
            send(k, b, at.up, 3, when=above)
            send(k, b, at.down, 4, when=below)
            send(k, b, at.sib, 0)
        arrived(k, z_block)
        send(k, z_block, at.up, 3, when=above)
        send(k, z_block, at.down, 4, when=below)
        send(k, z_block, at.sib, 0)

    def rise(k, s):
        lower = at.z - s >= 0
        upper = at.z + s <= PLANES - 1
        for there, level, onward, target, kind in (
            (lower, at.z - s, above, at.up, 3),
            (upper, at.z + s, below, at.down, 4),
        ):
            for i in range(4):
                b = at.c * CHIPS + 4 * level + i

                @pl.when(there)
                def _():
                    arrived(k, b)

                send(k, b, target, kind, when=there & onward)
                send(k, b, at.sib, 0, when=there)

    def norm_step(m):
        rows = pl.ds(m * block, block)
        values, _ = normalize(tok_ref[rows].astype(f32))
        unit[rows] = values
        unit_t[:, rows] = values.astype(bf16).T

    at.barrier()
    own_sends(0)
    norm_step(0)
    norm_step(1)
    plane(0, 0)
    column(0, 1)
    norm_step(2)
    norm_step(3)
    plane(0, 1)
    column(0, 2)
    plane(0, 2)
    column(0, 3)
    own_sends(1)
    plane(0, 3)
    norm_step(4)
    norm_step(5)
    for j in range(PLANES):
        corner(0, j)
    own_sends(2)
    norm_step(6)
    norm_step(7)
    unit_copy = pltpu.make_async_copy(unit_t, unit_hbm, copy_sem.at[slots])
    unit_copy.start()
    others(0)

    def strip(i):
        return pl.ds(pl.multiple_of(i * 2 * SHARD, 2 * SHARD), 2 * SHARD)

    def build_q(i, carry):
        first = gq[i].astype(f32)
        second = gq[CHIPS + i].astype(f32)
        fq[strip(i), :half_q] = jnp.concatenate(
            [first[:SHARD, :half_q], second[:SHARD, :half_q]], axis=0
        ).astype(bf16)
        fq[strip(i), half_q:] = jnp.concatenate(
            [first[SHARD:, :half_q], second[SHARD:, :half_q]], axis=0
        ).astype(bf16)
        return carry

    def build_oi(i, carry):
        first = goi[i].astype(f32)
        second = goi[CHIPS + i].astype(f32)
        fo[strip(i)] = jnp.concatenate([first[:SHARD], second[:SHARD]], axis=0).astype(bf16)
        fi[strip(i)] = jnp.concatenate([first[SHARD:], second[SHARD:]], axis=0).astype(bf16)
        return carry

    def build_b(i, carry):
        first = gb[i].astype(f32)
        second = gb[CHIPS + i].astype(f32)
        fb[strip(i), :half] = jnp.concatenate([first[:SHARD], second[:SHARD]], axis=0).astype(bf16)
        fb[strip(i), half:] = jnp.concatenate([first[SHARD:], second[SHARD:]], axis=0).astype(bf16)
        return carry

    lax.fori_loop(0, CHIPS, build_q, 0)
    fq_copy = pltpu.make_async_copy(fq, fq_hbm, copy_sem.at[slots + 1])
    fq_copy.start()
    for part in range(3):
        columns = slice(part * width, (part + 1) * width)
        fq_t[columns] = fq[:, columns].T

    column_at = lax.broadcasted_iota(jnp.int32, (128, width), 1)
    entry = lax.broadcasted_iota(jnp.int32, (128, width), 0)
    spread = jnp.where(lax.rem(column_at, SHARD) == entry, 1.0, 0.0).astype(bf16)
    stacked = jnp.concatenate([gq[p, :16, half_q:] for p in range(DEVICES)], axis=0)
    wide = dot(stacked, spread, 1, 0)
    total = jnp.zeros((16, width), f32)
    column_at = lax.broadcasted_iota(jnp.int32, (16, width), 1)
    for p in range(DEVICES):
        first = SHARD * ((p % CHIPS) * 2 + p // CHIPS)
        mine = (column_at >= first) & (column_at < first + SHARD)
        total = total + jnp.where(mine, wide[16 * p : 16 * p + 16], 0.0)
    vec_ref[...] = total
    bias[:width] = jnp.broadcast_to(total[2:3], (128, width)).T
    bias[width : 2 * width] = jnp.zeros((width, 128), f32)
    bias[2 * width :] = jnp.broadcast_to(total[3:4], (128, width)).T
    gain, shift = total[0:1], total[1:2]

    copies = []

    def qkv_step(m):
        normed = (unit[m * block : (m + 1) * block] * gain + shift).astype(bf16)

        def part_step(part, carry):
            rows = pl.ds(pl.multiple_of(part * width, width), width)
            result = dot(fq_t[rows], normed, 1, 1)
            added = bias[rows]
            qkv[m, rows] = (result + jnp.concatenate([added] * (block // 128), axis=1)).astype(
                bf16
            )
            return carry

        lax.fori_loop(0, 3, part_step, 0)
        copy = pltpu.make_async_copy(qkv.at[m], qkv_hbm.at[m], copy_sem.at[m])
        copy.start()
        copies.append(copy)

    plane(1, 0)
    column(1, 1)
    qkv_step(0)
    plane(1, 1)
    column(1, 2)
    flat(2)
    qkv_step(1)
    plane(1, 2)
    column(1, 3)
    rise(2, 1)
    plane(1, 3)
    qkv_step(2)
    rise(2, 2)
    qkv_step(3)
    rise(2, 3)
    qkv_step(4)
    for j in range(PLANES):
        corner(1, j)
    qkv_step(5)
    qkv_step(6)
    qkv_step(7)
    others(1)
    lax.fori_loop(0, CHIPS, build_oi, 0)
    fo_copy = pltpu.make_async_copy(fo, fo_hbm, copy_sem.at[slots + 2])
    fo_copy.start()
    fi_copy = pltpu.make_async_copy(fi, fi_hbm, copy_sem.at[slots + 3])
    fi_copy.start()
    others(2)
    lax.fori_loop(0, CHIPS, build_b, 0)
    fb_copy = pltpu.make_async_copy(fb, fb_hbm, copy_sem.at[slots + 4])
    fb_copy.start()
    for copy, when in pending:
        if when is None:
            copy.wait_send()
        else:
            pl.when(when)(copy.wait_send)
    for copy in copies + [unit_copy, fq_copy, fo_copy, fi_copy, fb_copy]:
        copy.wait()


def gather_and_project(small, w_qkv, w_out, w_in, w_back, tokens, slots):
    rows, width = tokens.shape
    block = rows // slots
    wide = 3 * width
    vmem = pl.BlockSpec(memory_space=pltpu.VMEM)
    anywhere = pl.BlockSpec(memory_space=pl.ANY)
    square = (width, width)
    return pl.pallas_call(
        gather_kernel,
        out_shape=[
            jax.ShapeDtypeStruct((slots, wide, block), bf16),
            jax.ShapeDtypeStruct((width, rows), bf16),
            jax.ShapeDtypeStruct((width, wide), bf16),
            jax.ShapeDtypeStruct(square, bf16),
            jax.ShapeDtypeStruct(square, bf16),
            jax.ShapeDtypeStruct(square, bf16),
            jax.ShapeDtypeStruct((16, width), f32),
        ],
        in_specs=[vmem] * 6,
        out_specs=[anywhere] * 6 + [vmem],
        scratch_shapes=[
            pltpu.VMEM((DEVICES, 2 * SHARD, wide // 2 + 128), bf16),
            pltpu.VMEM((DEVICES, 2 * SHARD, width), bf16),
            pltpu.VMEM((DEVICES, 2 * SHARD, width // 2), bf16),
            pltpu.VMEM((width, wide), bf16),
            pltpu.VMEM(square, bf16),
            pltpu.VMEM(square, bf16),
            pltpu.VMEM(square, bf16),
            pltpu.VMEM((wide, width), bf16),
            pltpu.VMEM((rows, width), f32),
            pltpu.VMEM((width, rows), bf16),
            pltpu.VMEM((slots, wide, block), bf16),
            pltpu.VMEM((wide, 128), f32),
            pltpu.SemaphoreType.DMA((3, CHIPS, 5)),
            pltpu.SemaphoreType.DMA((3, DEVICES)),
            pltpu.SemaphoreType.DMA((slots + 5,)),
        ],
        compiler_params=pltpu.CompilerParams(
            collective_id=0, has_side_effects=True, vmem_limit_bytes=58 * MIB
        ),
    )(small, w_qkv, w_out, w_in, w_back, tokens)


def middle_kernel(
    packed,
    head_dim,
    len_ref,
    qkv_ref,
    tok_ref,
    cot_ref,
    wout_ref,
    win_ref,
    wback_ref,
    vec_ref,
    mixed_ref,
    dmix_ref,
    dqkv_ref,
    gvec_ref,
    *rest,
):
    if packed:
        soi_ref, sb_ref, gout_ref, gin_ref, gback_ref, probs, ctx_s, linv_s, dctx_s = rest
    else:
        gout_ref, gin_ref, gback_ref, probs, ctx_s, linv_s, dctx_s = rest
    step = pl.program_id(0)
    block, width = tok_ref.shape
    slot = 32
    group = 4
    heads = width // head_dim
    span = group * head_dim
    scale = head_dim ** (-0.5)
    length = len_ref[step]

    @pl.when(step == 0)
    def _():
        gout_ref[...] = jnp.zeros_like(gout_ref)
        gin_ref[...] = jnp.zeros_like(gin_ref)
        gback_ref[...] = jnp.zeros_like(gback_ref)
        gvec_ref[...] = jnp.zeros_like(gvec_ref)

    def run(size):
        extra = (slot - head_dim, size)
        sub = lax.broadcasted_iota(jnp.int32, extra, 0)
        lane = lax.broadcasted_iota(jnp.int32, extra, 1)
        one_row = jnp.where(sub == 0, 1.0, 0.0).astype(f32)
        two_rows = jnp.where(sub <= 1, 1.0, 0.0).astype(f32)
        mask_row = jnp.where((sub == 0) & (lane >= length), masked_score, 0.0).astype(f32)

        def group_rows(base, g):
            return pl.ds(pl.multiple_of(base + g * span, span), span)

        def load(base, g):
            return qkv_ref[group_rows(base, g), :size].astype(f32)

        def place(j, rows):
            parts = []
            if j > 0:
                parts.append(jnp.zeros((slot * j, size), bf16))
            parts.append(rows)
            if j < group - 1:
                parts.append(jnp.zeros((slot * (group - 1 - j), size), bf16))
            return jnp.concatenate(parts, axis=0)

        def pieces(values):
            return [values[head_dim * j : head_dim * (j + 1)] for j in range(group)]

        def padded(values, tail):
            return [jnp.concatenate([p, tail], axis=0).astype(bf16) for p in pieces(values)]

        def forward(g):
            q = padded(load(0, g), one_row)
            k = jnp.concatenate(padded(load(width, g), mask_row), axis=0).T
            v = padded(load(2 * width, g), one_row)
            scores = [dot(k, place(j, q[j]), 1, 0) for j in range(group)]
            ps = []
            for j in range(group):
                peak = jnp.max(scores[j], axis=0, keepdims=True)
                p = jnp.exp2((scores[j] - peak) * (scale * log2_e)).astype(bf16)
                probs[g * group + j, :size, :size] = p
                ps.append(p)
            outs = []
            for j in range(group):
                o = dot(v[j], ps[j], 1, 0)
                inverse = 1.0 / o[head_dim : head_dim + 1]
                linv_s[g * group + j, :, :size] = jnp.broadcast_to(inverse, (8, size))
                outs.append(o[:head_dim] * inverse)
            ctx_s[group_rows(0, g), :size] = jnp.concatenate(outs, axis=0)

        def forward_step(i, carry):
            forward(2 * i)
            forward(2 * i + 1)
            return carry

        lax.fori_loop(0, heads // group // 2, forward_step, 0)

        live = (lax.broadcasted_iota(jnp.int32, (size, 1), 0) < length).astype(f32)
        out_bias, gain, shift = vec_ref[4:5], vec_ref[5:6], vec_ref[6:7]
        in_bias, back_bias = vec_ref[7:8], vec_ref[8:9]
        x = tok_ref[:size].astype(f32)
        dy = cot_ref[:size].astype(f32)
        ctx_t = ctx_s[:, :size].astype(bf16)
        attn = dot(ctx_t.T, wout_ref[...], 1, 0) + out_bias
        mixed = x + live * attn
        unit, factor = normalize(mixed)
        normed = (unit * gain + shift).astype(bf16)
        pre = dot(normed, win_ref[...], 1, 0) + in_bias
        cdf = 0.5 * (1.0 + lax.erf(pre * 0.7071067811865476))
        act = (pre * cdf).astype(bf16)
        slope = cdf + pre * jnp.exp(-0.5 * pre * pre) * 0.3989422804014327
        branch = dot(act, wback_ref[...], 1, 0) + back_bias
        mixed_ref[:size] = (mixed + live * branch).astype(bf16)
        d_ffn = live * dy
        gvec_ref[4] += fold_rows(d_ffn)
        d_ffn = d_ffn.astype(bf16)
        gback_ref[...] += dot(act.T, d_ffn, 1, 0)
        d_act = dot(d_ffn, wback_ref[...], 1, 1)
        d_pre = (d_act * slope).astype(bf16)
        gvec_ref[3] += fold_rows(d_pre.astype(f32))
        gin_ref[...] += dot(normed.T, d_pre, 1, 0)
        d_normed = dot(d_pre, win_ref[...], 1, 1)
        gvec_ref[1] += fold_rows(d_normed * unit)
        gvec_ref[2] += fold_rows(d_normed)
        d_mixed = dy + norm_backward(d_normed, gain, unit, factor)
        dmix_ref[:size] = d_mixed
        d_attn = (live * d_mixed).astype(bf16)
        gvec_ref[0] += fold_rows(d_attn.astype(f32))
        gout_ref[...] += dot(ctx_t, d_attn, 1, 0)
        dctx_s[:, :size] = dot(wout_ref[...], d_attn, 1, 1).astype(bf16)

        def backward(g):
            q = padded(load(0, g), one_row)
            k = padded(load(width, g), one_row)
            v = jnp.concatenate(padded(load(2 * width, g), two_rows), axis=0).T
            d_out = pieces(dctx_s[group_rows(0, g), :size].astype(f32))
            out = pieces(ctx_s[group_rows(0, g), :size])
            ds = []
            for j in range(group):
                d = d_out[j] * linv_s[g * group + j, :1, :size]
                inner = -jnp.sum(d * out[j], axis=0, keepdims=True)
                high = inner.astype(bf16).astype(f32)
                rest_rows = jnp.zeros((slot - head_dim - 2, size), f32)
                tail = jnp.concatenate([high, inner - high, rest_rows], axis=0)
                ds.append(jnp.concatenate([d, tail], axis=0).astype(bf16))
            d_probs = [dot(v, place(j, ds[j]), 1, 0) for j in range(group)]
            ps = [probs[g * group + j, :size, :size] for j in range(group)]
            d_scores = [(ps[j].astype(f32) * d_probs[j]).astype(bf16) for j in range(group)]
            d_v = [dot(ds[j], ps[j], 1, 1)[:head_dim] for j in range(group)]
            d_q = [dot(k[j], d_scores[j], 1, 0)[:head_dim] * scale for j in range(group)]
            d_k = [dot(q[j], d_scores[j], 1, 1)[:head_dim] * scale for j in range(group)]
            for base, parts in ((0, d_q), (width, d_k), (2 * width, d_v)):
                rows = group_rows(base, g)
                dqkv_ref[rows, :size] = jnp.concatenate(parts, axis=0).astype(bf16)

        def backward_step(i, carry):
            backward(2 * i)
            backward(2 * i + 1)
            return carry

        lax.fori_loop(0, heads // group // 2, backward_step, 0)

        if size < block:
            mixed_ref[size:] = tok_ref[size:]
            dmix_ref[size:] = cot_ref[size:].astype(f32)
            dqkv_ref[:, size:] = jnp.zeros((3 * width, block - size), bf16)

    half = block // 2

    @pl.when(length == 0)
    def _():
        mixed_ref[...] = tok_ref[...]
        dmix_ref[...] = cot_ref[...].astype(f32)
        dqkv_ref[...] = jnp.zeros_like(dqkv_ref)

    @pl.when((length > 0) & (length <= half))
    def _():
        run(half)

    @pl.when(length > half)
    def _():
        run(block)

    if packed:

        @pl.when(step == pl.num_programs(0) - 1)
        def _():
            columns = width // 2
            for i in range(DEVICES):
                p = (i % 2) * CHIPS + i // 2
                rows = slice(SHARD * i, SHARD * (i + 1))
                soi_ref[p] = jnp.concatenate([gout_ref[rows], gin_ref[rows]], axis=0).astype(bf16)
                sb_ref[p] = jnp.concatenate(
                    [gback_ref[rows, :columns], gback_ref[rows, columns:]], axis=0
                ).astype(bf16)


def middle(mol_len, qkv, tokens, cotangent, w_out, w_in, w_back, vectors, packed):
    slots = mol_len.shape[0]
    rows, width = tokens.shape
    block = rows // slots
    square = (width, width)

    def whole(shape):
        return pl.BlockSpec(shape, lambda m, lengths: (0,) * len(shape))

    by_rows = pl.BlockSpec((block, width), lambda m, lengths: (m, 0))
    out_specs = [
        by_rows,
        by_rows,
        pl.BlockSpec((3 * width, block), lambda m, lengths: (0, m)),
        whole((5, 8, width)),
    ]
    out_shape = [
        jax.ShapeDtypeStruct((rows, width), bf16),
        jax.ShapeDtypeStruct((rows, width), f32),
        jax.ShapeDtypeStruct((3 * width, rows), bf16),
        jax.ShapeDtypeStruct((5, 8, width), f32),
    ]
    scratch = [
        pltpu.VMEM((HEADS, block, block), bf16),
        pltpu.VMEM((width, block), f32),
        pltpu.VMEM((HEADS, 8, block), f32),
        pltpu.VMEM((width, block), bf16),
    ]
    if packed:
        shapes = [(DEVICES, 2 * SHARD, width), (DEVICES, 2 * SHARD, width // 2)]
        out_specs += [whole(s) for s in shapes]
        out_shape += [jax.ShapeDtypeStruct(s, bf16) for s in shapes]
        scratch = [pltpu.VMEM(square, f32)] * 3 + scratch
    else:
        out_specs += [whole(square)] * 3
        out_shape += [jax.ShapeDtypeStruct(square, f32)] * 3
    return pl.pallas_call(
        functools.partial(middle_kernel, packed, width // HEADS),
        grid_spec=pltpu.PrefetchScalarGridSpec(
            num_scalar_prefetch=1,
            grid=(slots,),
            in_specs=[
                pl.BlockSpec((None, 3 * width, block), lambda m, lengths: (m, 0, 0)),
                by_rows,
                by_rows,
                whole(square),
                whole(square),
                whole(square),
                whole((16, width)),
            ],
            out_specs=out_specs,
            scratch_shapes=scratch,
        ),
        out_shape=out_shape,
        compiler_params=pltpu.CompilerParams(vmem_limit_bytes=58 * MIB),
    )(mol_len, qkv, tokens, cotangent, w_out, w_in, w_back, vectors)


def scatter_kernel(
    soi_hbm,
    sb_hbm,
    dqkv_hbm,
    unit_hbm,
    fq_hbm,
    tok_hbm,
    dmix_hbm,
    vec_ref,
    gvec_ref,
    grad_hbm,
    gq_ref,
    go_ref,
    gi_ref,
    gb_ref,
    gs_ref,
    sq,
    soi,
    sb,
    rq_sib,
    roi_sib,
    rb_sib,
    rq,
    roi,
    rb_flat,
    rb_up,
    rb_down,
    dqkv,
    unit_t,
    fq,
    tok,
    dmix,
    grad,
    gain_wide,
    shift_wide,
    small_wide,
    sums,
    send_sem,
    recv_sem,
    copy_sem,
):
    at = Place()
    rows, width = tok.shape
    wide = 3 * width
    half_q = wide // 2
    half = width // 2
    slots = 8
    block = rows // slots
    mine = at.c * CHIPS
    own = at.block(at.c, at.z, at.y, at.x)
    level_rows = 8 * SHARD

    def local(src, dst, i):
        copy = pltpu.make_async_copy(src, dst, copy_sem.at[i])
        copy.start()
        return copy

    oi_in = local(soi_hbm, soi, 0)
    b_in = local(sb_hbm, sb, 1)
    unit_in = local(unit_hbm, unit_t, 2)
    dqkv_in = local(dqkv_hbm, dqkv, 3)
    fq_in = local(fq_hbm, fq, 4)
    tok_in = local(tok_hbm, tok, 5)
    dmix_in = local(dmix_hbm, dmix, 6)

    pending = []

    def remote(src, dst, target, k, kind, j):
        return pltpu.make_async_remote_copy(
            src_ref=src,
            dst_ref=dst,
            send_sem=send_sem.at[k, kind, j],
            recv_sem=recv_sem.at[k, kind, j],
            device_id=(target,),
            device_id_type=MESH,
        )

    def send(copy, when=None):
        pending.append((copy, when))
        if when is None:
            copy.start()
        else:
            pl.when(when)(copy.start)

    def add(slab, p, other, q):
        slab[p] = (slab[p].astype(f32) + other[q].astype(f32)).astype(bf16)

    slabs = (sq, soi, sb)
    from_sib = (rq_sib, roi_sib, rb_sib)
    steps = (rq, roi)

    def x_type(z):
        return at.block(at.c, z, at.y, 1 - at.x)

    def y_type(z):
        return at.block(at.c, z, 1 - at.y, at.x)

    def corner_type(z):
        return at.block(at.c, z, 1 - at.y, 1 - at.x)

    def sib_copy(k, j):
        return remote(
            slabs[k].at[pl.ds((1 - at.c) * CHIPS + 4 * j, 4)],
            from_sib[k].at[pl.ds(4 * j, 4)],
            at.sib,
            k,
            0,
            j,
        )

    def sib_send(k, j):
        send(sib_copy(k, j))

    def sib_add(k, j):
        sib_copy(k, j).wait_recv()

        def body(i, carry):
            add(slabs[k], mine + 4 * j + i, from_sib[k], 4 * j + i)
            return carry

        lax.fori_loop(0, 4, body, 0)

    def step_copy(k, kind, j, src, target):
        return remote(
            slabs[k].at[pl.ds(src, 1)], steps[k].at[pl.ds(4 * (kind - 1) + j, 1)], target, k, kind, j
        )

    def corner_send(k, j):
        target = at.yn if j % 2 == 0 else at.xn
        send(step_copy(k, 1, j, corner_type(j), target))
        if j % 2 == 0:
            send(step_copy(k, 3, j, y_type(j), at.yn))
        else:
            send(step_copy(k, 2, j, x_type(j), at.xn))

    def corner_add(k, j):
        step_copy(k, 1, j, corner_type(j), at.yn).wait_recv()
        if j % 2 == 0:
            add(slabs[k], x_type(j), steps[k], j)
            send(step_copy(k, 2, j, x_type(j), at.xn))
        else:
            add(slabs[k], y_type(j), steps[k], j)
            send(step_copy(k, 3, j, y_type(j), at.yn))

    def plane_add(k, j):
        p = at.block(at.c, j, at.y, at.x)
        step_copy(k, 2, j, p, at.xn).wait_recv()
        step_copy(k, 3, j, p, at.yn).wait_recv()
        total = slabs[k][p].astype(f32) + steps[k][4 + j].astype(f32) + steps[k][8 + j].astype(f32)
        slabs[k][p] = total.astype(bf16)

    def climb(k, j, hop):
        p = at.block(at.c, j, at.y, at.x)
        for z, kind, target, further in (
            (j - hop, 4, at.up, j - hop - 1 >= 0),
            (j + hop, 5, at.down, j + hop + 1 <= PLANES - 1),
        ):
            if 0 <= z <= PLANES - 1:
                here = at.z == z
                if further:

                    @pl.when(here)
                    def _():
                        step_copy(k, kind, j, p, target).wait_recv()
                        add(slabs[k], p, steps[k], 4 * (kind - 1) + j)

                send(step_copy(k, kind, j, p, target), here)

    def land(k, j):
        p = at.block(at.c, j, at.y, at.x)
        for kind, target, there in ((4, at.up, j > 0), (5, at.down, j < PLANES - 1)):
            if there:

                @pl.when(at.z == j)
                def _():
                    step_copy(k, kind, j, p, target).wait_recv()
                    add(slabs[k], p, steps[k], 4 * (kind - 1) + j)

    def group_copy(kind, j, target):
        buffer = rb_up if kind == 4 else rb_down
        return remote(
            sb.at[pl.ds(mine + 4 * j, 4)], buffer.at[pl.ds(4 * j, 4)], target, 2, kind, j
        )

    def group_add(buffer, j):
        def body(i, carry):
            add(sb, mine + 4 * j + i, buffer, 4 * j + i)
            return carry

        lax.fori_loop(0, 4, body, 0)

    def group_climb(j, hop):
        for z, kind, target, further, buffer in (
            (j - hop, 4, at.up, j - hop - 1 >= 0, rb_up),
            (j + hop, 5, at.down, j + hop + 1 <= PLANES - 1, rb_down),
        ):
            if 0 <= z <= PLANES - 1:
                here = at.z == z
                if further:

                    @pl.when(here)
                    def _():
                        group_copy(kind, j, target).wait_recv()
                        group_add(buffer, j)

                send(group_copy(kind, j, target), here)

    def group_land(j):
        for kind, target, there, buffer in (
            (4, at.up, j > 0, rb_up),
            (5, at.down, j < PLANES - 1, rb_down),
        ):
            if there:

                @pl.when(at.z == j)
                def _():
                    group_copy(kind, j, target).wait_recv()
                    group_add(buffer, j)

    def flat_copy(kind, src, target):
        return remote(sb.at[pl.ds(src, 1)], rb_flat.at[pl.ds(kind - 1, 1)], target, 2, kind, 0)

    even = lax.rem(at.z, 2) == 0
    odd = jnp.logical_not(even)

    def flat_start():
        z = at.z
        send(flat_copy(1, corner_type(z), at.yn), even)
        send(flat_copy(1, corner_type(z), at.xn), odd)
        send(flat_copy(3, y_type(z), at.yn), even)
        send(flat_copy(2, x_type(z), at.xn), odd)

    def flat_corner():
        z = at.z
        flat_copy(1, own, at.yn).wait_recv()

        @pl.when(even)
        def _():
            add(sb, x_type(z), rb_flat, 0)

        @pl.when(odd)
        def _():
            add(sb, y_type(z), rb_flat, 0)

        send(flat_copy(2, x_type(z), at.xn), even)
        send(flat_copy(3, y_type(z), at.yn), odd)

    def flat_end():
        flat_copy(2, own, at.xn).wait_recv()
        flat_copy(3, own, at.yn).wait_recv()
        total = sb[own].astype(f32) + rb_flat[1].astype(f32) + rb_flat[2].astype(f32)
        gb_ref[:, :half] = total[:SHARD]
        gb_ref[:, half:] = total[SHARD:]

    def prepare():
        gain_wide[...] = jnp.broadcast_to(vec_ref[0:1], (128, width)).T
        shift_wide[...] = jnp.broadcast_to(vec_ref[1:2], (128, width)).T
        ones = jnp.ones((16, rows), bf16)
        for part in range(3):
            columns = slice(part * width, (part + 1) * width)
            sums[:, columns] = dot(ones, dqkv[columns], 1, 1)[:8]
        lines = [jnp.zeros((2, width), f32), sums[0:1, :width], sums[0:1, 2 * width :]]
        lines += [jnp.sum(gvec_ref[i], axis=0, keepdims=True) for i in range(5)]
        lines.append(jnp.zeros((128 - 9, width), f32))
        small_wide[...] = jnp.concatenate(lines, axis=0).T

    def weight_grad(j):
        lines = pl.ds(j * level_rows, level_rows)
        left = unit_t[lines]
        lane = lax.broadcasted_iota(jnp.int32, (level_rows, 128), 1)
        gain_sum = jnp.zeros((level_rows, 1), f32)
        shift_sum = jnp.zeros((level_rows, 1), f32)
        pieces = []
        for part in range(3):
            columns = slice(part * width, (part + 1) * width)
            product = dot(left, dqkv[columns], 1, 1)
            weight = fq[lines, columns].astype(f32)
            line = sums[0:1, columns]
            gain_sum += jnp.sum(weight * product, axis=1, keepdims=True)
            shift_sum += jnp.sum(weight * line, axis=1, keepdims=True)
            gain = jnp.concatenate([gain_wide[lines]] * (width // 128), axis=1)
            shift = jnp.concatenate([shift_wide[lines]] * (width // 128), axis=1)
            pieces.append(gain * product + shift * line)
        result = jnp.concatenate(pieces, axis=1)
        small = small_wide[lines]
        small = jnp.where(lane == 0, gain_sum, jnp.where(lane == 1, shift_sum, small))
        blank = jnp.zeros((SHARD, 128), f32)
        for i in range(8):
            p = (i % 2) * CHIPS + 4 * j + i // 2
            some = slice(SHARD * i, SHARD * (i + 1))
            top = jnp.concatenate([result[some, :half_q], small[some]], axis=1)
            bottom = jnp.concatenate([result[some, half_q:], blank], axis=1)
            sq[p] = jnp.concatenate([top, bottom], axis=0).astype(bf16)

    grads = []

    def input_grad(m):
        some = slice(m * block, (m + 1) * block)
        d_normed = dot(fq[...], dqkv[:, some], 1, 0).T
        unit, factor = normalize(tok[some].astype(f32))
        share = norm_backward(d_normed, vec_ref[0:1], unit, factor)
        grad[some] = (dmix[some] + share).astype(bf16)
        grads.append(local(grad.at[pl.ds(m * block, block)], grad_hbm.at[pl.ds(m * block, block)], 7 + m))

    at.barrier()
    oi_in.wait()
    for j in range(PLANES):
        sib_send(1, j)
    b_in.wait()
    for j in range(PLANES):
        sib_send(2, j)
    unit_in.wait()
    dqkv_in.wait()
    fq_in.wait()
    for j in range(PLANES):
        sib_add(1, j)
        corner_send(1, j)
    for j in range(PLANES):
        sib_add(2, j)
    for j in range(PLANES):
        group_climb(j, 3)
    prepare()
    for j in range(PLANES):
        corner_add(1, j)
    for j in range(PLANES):
        group_climb(j, 2)
    weight_grad(0)
    sib_send(0, 0)
    for j in range(PLANES):
        plane_add(1, j)
        climb(1, j, 3)
    for j in range(PLANES):
        group_climb(j, 1)
    weight_grad(3)
    sib_send(0, 3)
    sib_add(0, 0)
    corner_send(0, 0)
    for j in range(PLANES):
        climb(1, j, 2)
    for j in range(PLANES):
        group_land(j)
    flat_start()
    weight_grad(1)
    sib_send(0, 1)
    sib_add(0, 3)
    corner_send(0, 3)
    corner_add(0, 0)
    for j in range(PLANES):
        climb(1, j, 1)
    flat_corner()
    weight_grad(2)
    sib_send(0, 2)
    sib_add(0, 1)
    corner_send(0, 1)
    corner_add(0, 3)
    plane_add(0, 0)
    climb(0, 0, 3)
    tok_in.wait()
    dmix_in.wait()
    input_grad(0)
    sib_add(0, 2)
    corner_send(0, 2)
    corner_add(0, 1)
    plane_add(0, 3)
    climb(0, 3, 3)
    climb(0, 0, 2)
    input_grad(1)
    corner_add(0, 2)
    plane_add(0, 1)
    climb(0, 1, 2)
    climb(0, 3, 2)
    climb(0, 0, 1)
    input_grad(2)
    plane_add(0, 2)
    climb(0, 2, 2)
    climb(0, 1, 1)
    climb(0, 3, 1)
    input_grad(3)
    climb(0, 2, 1)
    for j in range(PLANES):
        land(1, j)
    input_grad(4)
    flat_end()
    input_grad(5)
    input_grad(6)
    input_grad(7)
    for j in range(PLANES):
        land(0, j)
    last = sq[own].astype(f32)
    gq_ref[:, :half_q] = last[:SHARD, :half_q]
    gq_ref[:, half_q:] = last[SHARD:, :half_q]
    gs_ref[...] = last[:SHARD, half_q:]
    last = soi[own].astype(f32)
    go_ref[...] = last[:SHARD]
    gi_ref[...] = last[SHARD:]
    for copy, when in pending:
        if when is None:
            copy.wait_send()
        else:
            pl.when(when)(copy.wait_send)
    for copy in grads:
        copy.wait()


def scatter(soi, sb, dqkv, unit_t, full_qkv, tokens, d_mixed, vectors, sums):
    rows, width = tokens.shape
    wide = 3 * width
    vmem = pl.BlockSpec(memory_space=pltpu.VMEM)
    anywhere = pl.BlockSpec(memory_space=pl.ANY)
    tall = 2 * SHARD
    widths = (wide // 2 + 128, width, width // 2)
    return pl.pallas_call(
        scatter_kernel,
        out_shape=[
            jax.ShapeDtypeStruct((rows, width), bf16),
            jax.ShapeDtypeStruct((SHARD, wide), f32),
            jax.ShapeDtypeStruct((SHARD, width), f32),
            jax.ShapeDtypeStruct((SHARD, width), f32),
            jax.ShapeDtypeStruct((SHARD, width), f32),
            jax.ShapeDtypeStruct((SHARD, 128), f32),
        ],
        in_specs=[anywhere] * 7 + [vmem] * 2,
        out_specs=[anywhere] + [vmem] * 5,
        scratch_shapes=[pltpu.VMEM((DEVICES, tall, w), bf16) for w in widths]
        + [pltpu.VMEM((CHIPS, tall, w), bf16) for w in widths]
        + [pltpu.VMEM((5 * PLANES, tall, w), bf16) for w in widths[:2]]
        + [
            pltpu.VMEM((3, tall, width // 2), bf16),
            pltpu.VMEM((CHIPS, tall, width // 2), bf16),
            pltpu.VMEM((CHIPS, tall, width // 2), bf16),
            pltpu.VMEM((wide, rows), bf16),
            pltpu.VMEM((width, rows), bf16),
            pltpu.VMEM((width, wide), bf16),
            pltpu.VMEM((rows, width), bf16),
            pltpu.VMEM((rows, width), f32),
            pltpu.VMEM((rows, width), bf16),
            pltpu.VMEM((width, 128), f32),
            pltpu.VMEM((width, 128), f32),
            pltpu.VMEM((width, 128), f32),
            pltpu.VMEM((8, wide), f32),
            pltpu.SemaphoreType.DMA((3, 6, PLANES)),
            pltpu.SemaphoreType.DMA((3, 6, PLANES)),
            pltpu.SemaphoreType.DMA((15,)),
        ],
        compiler_params=pltpu.CompilerParams(
            collective_id=1, has_side_effects=True, vmem_limit_bytes=60 * MIB
        ),
    )(soi, sb, dqkv, unit_t, full_qkv, tokens, d_mixed, vectors, sums)


def on_one_plan(tokens, mol_len, cotangent, vectors, w_qkv, w_out, w_in, w_back):
    slots = mol_len.shape[0]
    small = jnp.pad(jnp.stack(vectors), ((0, 16 - len(vectors)), (0, 128 - SHARD)))
    qkv, unit_t, full_qkv, full_out, full_in, full_back, lines = gather_and_project(
        small, w_qkv, w_out, w_in, w_back, tokens, slots
    )
    mixed_out, d_mixed, dqkv, sums, soi, sb = middle(
        mol_len, qkv, tokens, cotangent, full_out, full_in, full_back, lines, True
    )
    token_grad, g_qkv, g_out, g_in, g_back, g_small = scatter(
        soi, sb, dqkv, unit_t, full_qkv, tokens, d_mixed, lines, sums
    )
    g_small = g_small.T
    return mixed_out, token_grad, [g_small[i] for i in range(9)], g_qkv, g_out, g_in, g_back


def on_any_plan(tokens, mol_len, cotangent, vectors, w_qkv, w_out, w_in, w_back):
    slots = mol_len.shape[0]
    rows, width = tokens.shape

    def gather(array, axis):
        return lax.all_gather(array, "fsdp", axis=axis, tiled=True)

    lines = gather(jnp.stack(vectors), 1).astype(f32)
    lines = jnp.pad(lines, ((0, 16 - len(vectors)), (0, 0)))
    full_qkv, full_out, full_in, full_back = (
        gather(w, 0) for w in (w_qkv, w_out, w_in, w_back)
    )
    unit, factor = normalize(tokens.astype(f32))
    normed = (unit * lines[0] + lines[1]).astype(bf16)
    qkv = jnp.dot(normed, full_qkv, preferred_element_type=f32)
    qkv = (qkv + jnp.concatenate([lines[2], jnp.zeros_like(lines[2]), lines[3]])).astype(bf16)
    qkv = qkv.reshape(slots, rows // slots, 3 * width).transpose(0, 2, 1)
    mixed_out, d_mixed, dqkv, sums, g_out, g_in, g_back = middle(
        mol_len, qkv, tokens, cotangent, full_out, full_in, full_back, lines, False
    )
    g_qkv = jnp.einsum("rf,dr->fd", normed, dqkv, preferred_element_type=f32)
    d_normed = jnp.einsum("dr,fd->rf", dqkv, full_qkv, preferred_element_type=f32)
    totals = jnp.sum(dqkv.astype(f32), axis=1)
    small = [jnp.sum(d_normed * unit, axis=0), jnp.sum(d_normed, axis=0)]
    small += [totals[:width], totals[2 * width :]]
    small += [jnp.sum(sums[i], axis=0) for i in range(5)]
    share = norm_backward(d_normed, lines[0], unit, factor)
    token_grad = (d_mixed + share).astype(bf16)

    def scatter_sum(array, axis):
        return lax.psum_scatter(array, "fsdp", scatter_dimension=axis, tiled=True)

    small = scatter_sum(jnp.stack(small), 1)
    return (
        mixed_out,
        token_grad,
        [small[i] for i in range(9)],
        *(scatter_sum(g, 0) for g in (g_qkv, g_out, g_in, g_back)),
    )


def per_device(
    devices,
    tokens,
    mol_len,
    cotangent,
    ln1_gain,
    ln1_bias,
    w_qkv,
    q_bias,
    v_bias,
    w_out,
    out_bias,
    ln2_gain,
    ln2_bias,
    w_in,
    in_bias,
    w_back,
    back_bias,
):
    vectors = [
        ln1_gain,
        ln1_bias,
        q_bias,
        v_bias,
        out_bias,
        ln2_gain,
        ln2_bias,
        in_bias,
        back_bias,
    ]
    known = devices == DEVICES and w_qkv.shape[0] == SHARD
    plan = on_one_plan if known else on_any_plan
    mixed_out, token_grad, small, g_qkv, g_out, g_in, g_back = plan(
        tokens, mol_len, cotangent, vectors, w_qkv, w_out, w_in, w_back
    )
    return (
        mixed_out,
        token_grad,
        small[0],
        small[1],
        g_qkv,
        small[2],
        small[3],
        g_out,
        small[4],
        small[5],
        small[6],
        g_in,
        small[7],
        g_back,
        small[8],
    )


def solution(mesh):
    line, matrix = P("fsdp"), P("fsdp", None)
    return jax.shard_map(
        functools.partial(per_device, mesh.shape["fsdp"]),
        mesh=mesh,
        in_specs=(
            matrix,
            line,
            matrix,
            line,
            line,
            matrix,
            line,
            line,
            matrix,
            line,
            line,
            line,
            matrix,
            line,
            matrix,
            line,
        ),
        out_specs=(
            matrix,
            matrix,
            line,
            line,
            matrix,
            line,
            line,
            matrix,
            line,
            line,
            line,
            matrix,
            line,
            matrix,
            line,
        ),
        check_vma=False,
    )
```

time: 767 us -> 248 us (0.32); the launches traced: 755 us -> 247 us
  matrix products: 406 us -> 0 us
  Pallas kernels: 0 us -> 235 us
  local copies, waits for them, and re-layouts: 150 us -> 10.4 us
  blocking collectives: 83.8 us -> 0 us
  other arithmetic: 63 us -> 0 us
  waiting for transfers between devices: 35.8 us -> 0 us
  between operations: 15.2 us -> 1.12 us
    dot_general x40 -> x0, matrix products: 406 us -> none  [the longest x4 93.5 us: group_backward(): jnp.einsum('bhqk,bqhd->bkhd', d_scores, q_group, preferred_element_type=j...]
    pallas_call x0 -> x3, Pallas kernels: none -> 235 us  [the longest x1 115 us: scatter(): pl.pallas_call(scatter_kernel, out_shape=[jax.ShapeDtypeStruct((rows, wid...]
    unnamed x2 -> x0, blocking collectives: 83.8 us -> none
    unnamed x129 -> x13, local copies, waits for them, and re-layouts: 66 us -> 6.41 us
    reduce_sum x13 -> x0, other arithmetic: 45 us -> none  [the longest x4 16.6 us: group_forward(): row_total = jnp.sum(weights, axis=-1, keepdims=True)]
    convert_element_type x7 -> x0, local copies, waits for them, and re-layouts: 25.6 us -> none  [the longest x1 4.64 us: per_device(): context_low = join_heads(context).astype(jnp.bfloat16)]
    all_gather x4 -> x0, waiting for transfers between devices: 19.8 us -> none  [the longest x1 19.2 us: per_device(): lax.all_gather(w_back, 'fsdp', axis=0, tiled=True)]
    while x40 -> x0, local copies, waits for them, and re-layouts: 18.8 us -> none
  transfers between devices with their start and end apart: 8 -> 0, of which waited for: 3 -> 0; matrix products, arithmetic and copies ran while one was open for 76% -> 0% of each run, Pallas kernels for 0% -> 0%
where the time goes in v1:
time: 248 us; the launch traced here: 247 us
  Pallas kernels  235 us (95%)
  local copies, waits for them, and re-layouts  10.4 us (4%)
    pallas_call x1, Pallas kernels, scatter(): pl.pallas_call(scatter_kernel, out_shape=[jax.ShapeDtypeStruct((rows, wid...  115 us
    pallas_call x1, Pallas kernels, gather_and_project(): pl.pallas_call(gather_kernel, out_shape=[jax.ShapeDtypeStruct((slots, wid...  67.3 us
    pallas_call x1, Pallas kernels, middle(): pl.pallas_call(functools.partial(middle_kernel, packed, width // HEADS),...  53.2 us
    unnamed x13, local copies, waits for them, and re-layouts  6.41 us

profile of v1, /device:TPU:0, one launch (start us, length us, event | category | flops | bytes accessed | tf_op | source)
XLA Modules:
  0.0 246.7 jit_solution(14613865941253334465)
XLA Ops:
  0.6 1.5 stack.39
  2.1 0.6 pad.4.small_ref
  2.7 67.3 %shard_map.271 = (bf16[8,2304,256]{2,1,0:T(8,128)(2,1)}, bf16[768,2048]{1,0:T(8,128)(2,1)}, bf16[768,2304]{1,0:T(8,128)(2,1)}, bf16[768,768]{1,0:T(8,128)(2,1)},...) custom-call(bf16[16,128]{1,0:T(8,128)(2,1)} %pad.4.small_ref, bf16[24,2304]{1,0:T(8,128)(2,1)} %wq_ref.1, ...), custom_call_target="tpu_custom_call" | custom-call | tf_op jit(solution)/shard_map/pallas_call | solution.py:399
  70.0 53.2 %shard_map.272 = (bf16[2048,768]{1,0:T(8,128)(2,1)}, f32[2048,768]{1,0:T(8,128)}, bf16[2304,2048]{1,0:T(8,128)(2,1)}, f32[5,8,768]{2,1,0:T(8,128)}, bf16[32,48,7...) custom-call(s32[8]{0:T(128)} %len_ref.1, bf16[8,2304,256]{2,1,0:T(8,128)(2,1)} %get-tuple-element.34.qkv_ref, ...), custom_call_target="tpu_custom_call" | custom-call | tf_op jit(solution)/shard_map/pallas_call | solution.py:663
  123.2 114.7 %shard_map.273 = (bf16[2048,768]{1,0:T(8,128)(2,1)}, f32[24,2304]{1,0:T(8,128)}, f32[24,768]{1,0:T(8,128)}, f32[24,768]{1,0:T(8,128)}, f32[24,768]{1,0:T(8,128)}, /*index=5*/f32[24,128]{1,0:T(8,128)}) custom-call(bf16[32,48,768]{2,1,0:T(8,128)(2,1)} %get-tuple-element.40.soi_hbm, bf16[32,48,384]{2,1,0:T(8,128)(2,1)} %get-tuple-element.41.sb_hbm, ...), custom_call_target="tpu_custom_call" | custom-call | tf_op jit(solution)/shard_map/pallas_call | solution.py:1096
  237.9 1.9 slice_reduce_fusion
  239.8 0.0 copy-start
  239.8 0.0 copy-start.3
  239.8 0.0 copy-start.2
  239.8 0.0 copy-start.1
  239.8 3.8 %copy.36 = bf16[2048,768]{1,0:T(8,128)(2,1)} copy(bf16[2048,768]{1,0:T(8,128)(2,1)} %get-tuple-element.78) | data formatting | bytes 6291456
  243.6 0.0 copy-done
  243.6 0.7 copy.37
  244.3 0.0 copy-done.3
  244.3 0.6 copy.38
  245.0 0.0 copy-done.2
  245.0 0.6 copy.39
  245.6 0.0 copy-done.1
  245.6 0.6 copy.40
Async XLA Ops:
  239.8 3.8 %copy-start = (f32[24,2304]{1,0:T(8,128)S(1)}, f32[24,2304]{1,0:T(8,128)}, u32[]{:S(2)}) copy-start(f32[24,2304]{1,0:T(8,128)} %get-tuple-element.81) | copy-start | bytes 663556
  239.8 4.5 %copy-start.3 = (f32[24,768]{1,0:T(8,128)S(1)}, f32[24,768]{1,0:T(8,128)}, u32[]{:S(2)}) copy-start(f32[24,768]{1,0:T(8,128)} %get-tuple-element.84) | copy-start | bytes 221188
  239.8 5.1 %copy-start.2 = (f32[24,768]{1,0:T(8,128)S(1)}, f32[24,768]{1,0:T(8,128)}, u32[]{:S(2)}) copy-start(f32[24,768]{1,0:T(8,128)} %get-tuple-element.88) | copy-start | bytes 221188
  239.8 5.8 %copy-start.1 = (f32[24,768]{1,0:T(8,128)S(1)}, f32[24,768]{1,0:T(8,128)}, u32[]{:S(2)}) copy-start(f32[24,768]{1,0:T(8,128)} %get-tuple-element.90) | copy-start | bytes 221188

commit v2 on v1

v2 whole, which is shorter than its diff:
```python
import functools

import jax
import jax.numpy as jnp
from jax import lax
from jax.experimental import pallas as pl
from jax.experimental.pallas import tpu as pltpu
from jax.sharding import PartitionSpec as P

HEADS = 32

bf16 = jnp.bfloat16
f32 = jnp.float32
eps = 1e-05
masked_score = -1e30
log2_e = 1.4426950408889634
MESH = pl.DeviceIdType.MESH
MIB = 1 << 20

PLANES = 4
CHIPS = 4 * PLANES
DEVICES = 2 * CHIPS
SHARD = 24


def dot(left, right, left_dim, right_dim):
    return lax.dot_general(
        left, right, (((left_dim,), (right_dim,)), ((), ())), preferred_element_type=f32
    )


def normalize(values):
    centred = values - jnp.mean(values, axis=-1, keepdims=True)
    factor = lax.rsqrt(jnp.mean(centred * centred, axis=-1, keepdims=True) + eps)
    return centred * factor, factor


def norm_backward(d_normed, gain, unit, factor):
    e = d_normed * gain
    inner = jnp.mean(e * unit, axis=-1, keepdims=True)
    return factor * (e - jnp.mean(e, axis=-1, keepdims=True) - unit * inner)


def fold_rows(values):
    rows, columns = values.shape
    return jnp.sum(values.reshape(rows // 8, 8, columns), axis=0)


class Place:
    def __init__(self):
        me = lax.axis_index("fsdp")
        self.me = me
        self.c = lax.rem(me, 2)
        self.x = lax.rem(me // 2, 2)
        self.y = lax.rem(me // 4, 2)
        self.z = me // 8
        self.sib = me + 1 - 2 * self.c
        self.xn = me + 2 - 4 * self.x
        self.yn = me + 4 - 8 * self.y

    def block(self, c, z, y, x):
        return ((c * PLANES + z) * 2 + y) * 2 + x

    def greet(self):
        sem = pltpu.get_barrier_semaphore()

        def signal(device):
            pl.semaphore_signal(sem, inc=1, device_id=(device,), device_id_type=MESH)

        for device in (self.sib, self.xn, self.yn):
            signal(device)
        for distance in range(1, PLANES):
            signal(lax.rem(self.me + 8 * distance, DEVICES))

    def await_all(self):
        pl.semaphore_wait(pltpu.get_barrier_semaphore(), 2 + PLANES)


def gather_kernel(
    small_ref,
    wq_ref,
    wo_ref,
    wi_ref,
    wb_ref,
    tok_ref,
    qkv_hbm,
    unit_hbm,
    fq_hbm,
    fo_hbm,
    fi_hbm,
    fb_hbm,
    vec_ref,
    gq,
    gr,
    fq,
    fo,
    fi,
    fb,
    fq_t,
    unit,
    unit_t,
    qkv,
    bias,
    send_sem,
    recv_sem,
    copy_sem,
):
    at = Place()
    at.greet()
    width = tok_ref.shape[1]
    slots, _, block = qkv.shape
    half_q = 3 * width // 2
    half = width // 2
    own = at.block(at.c, at.z, at.y, at.x)
    mine, theirs = at.c * CHIPS, (1 - at.c) * CHIPS
    slabs = ((gq, 0, 384), (gq, 384, 384), (gq, 768, 512), (gr, 0, 640), (gr, 640, 512))

    gq[own] = jnp.concatenate(
        [
            jnp.concatenate([wq_ref[:, :half_q], wq_ref[:, half_q:]], axis=0),
            jnp.concatenate([small_ref[...], jnp.zeros((2 * SHARD - 16, 128), bf16)], axis=0),
        ],
        axis=1,
    )
    gr[own] = jnp.concatenate(
        [
            jnp.concatenate([wo_ref[...], wi_ref[...]], axis=0),
            jnp.concatenate([wb_ref[:, :half], wb_ref[:, half:]], axis=0),
        ],
        axis=1,
    )

    def view(k, first, count):
        slab, column, columns = slabs[k]
        return slab.at[pl.ds(first, count), :, pl.ds(column, columns)]

    def remote(k, first, target, sem, count=1):
        return pltpu.make_async_remote_copy(
            src_ref=view(k, first, count),
            dst_ref=view(k, first, count),
            send_sem=send_sem.at[k],
            recv_sem=recv_sem.at[k, sem],
            device_id=(target,),
            device_id_type=MESH,
        )

    def send(k, b, target):
        remote(k, b, target, lax.rem(b, CHIPS)).start()

    def to_sib(k, b):
        remote(k, b, at.sib, CHIPS).start()

    def arrived(k, b):
        remote(k, b, at.sib, lax.rem(b, CHIPS)).wait_recv()

    def at_level(shift, body):
        level = at.z + shift
        if shift == 0:
            body(level)
        else:
            pl.when((level >= 0) & (level <= PLANES - 1))(lambda: body(level))

    def both(s):
        return (0,) if s == 0 else (-s, s)

    def own_plane(k):
        send(k, own, at.xn)
        send(k, own, at.yn)

    def own_column(k):
        for s in range(1, PLANES):
            for shift in both(s):
                at_level(shift, lambda level, shift=shift: send(k, own, at.me + 8 * shift))
        to_sib(k, own)

    def column(k, s):
        def body(level):
            b = at.block(at.c, level, at.y, at.x)
            arrived(k, b)
            send(k, b, at.xn)
            send(k, b, at.yn)
            to_sib(k, b)

        for shift in both(s):
            at_level(shift, body)

    def plane(k, s):
        def body(level):
            even = lax.rem(level, 2) == 0
            b = at.block(at.c, level, at.y, 1 - at.x)
            arrived(k, b)
            pl.when(even)(lambda: send(k, b, at.yn))
            to_sib(k, b)
            d = at.block(at.c, level, 1 - at.y, at.x)
            arrived(k, d)
            pl.when(jnp.logical_not(even))(lambda: send(k, d, at.xn))
            to_sib(k, d)

        for shift in both(s):
            at_level(shift, body)

    def corner(k):
        for j in range(PLANES):
            b = at.block(at.c, j, 1 - at.y, 1 - at.x)
            arrived(k, b)
            to_sib(k, b)

    def others(k):
        remote(k, theirs, at.sib, CHIPS, CHIPS).wait_recv()

    def norm_step(m):
        rows = pl.ds(m * block, block)
        values, _ = normalize(tok_ref[rows].astype(f32))
        unit[rows] = values
        unit_t[:, rows] = values.astype(bf16).T

    def strip(i):
        return pl.ds(pl.multiple_of(i * 2 * SHARD, 2 * SHARD), 2 * SHARD)

    def stack(first, second):
        return jnp.concatenate([first, second], axis=0).astype(bf16)

    def build_q():
        def body(i, carry):
            first = gq[i].astype(f32)
            second = gq[CHIPS + i].astype(f32)
            fq[strip(i), :half_q] = stack(first[:SHARD, :half_q], second[:SHARD, :half_q])
            fq[strip(i), half_q:] = stack(first[SHARD:, :half_q], second[SHARD:, :half_q])
            return carry

        lax.fori_loop(0, CHIPS, body, 0)
        out(fq, fq_hbm)

    def build_r():
        def body(i, carry):
            first = gr[i].astype(f32)
            second = gr[CHIPS + i].astype(f32)
            fo[strip(i)] = stack(first[:SHARD, :width], second[:SHARD, :width])
            fi[strip(i)] = stack(first[SHARD:, :width], second[SHARD:, :width])
            fb[strip(i), :half] = stack(first[:SHARD, width:], second[:SHARD, width:])
            fb[strip(i), half:] = stack(first[SHARD:, width:], second[SHARD:, width:])
            return carry

        lax.fori_loop(0, CHIPS, body, 0)
        out(fo, fo_hbm)
        out(fi, fi_hbm)
        out(fb, fb_hbm)

    copies = []

    def out(src, dst):
        copy = pltpu.make_async_copy(src, dst, copy_sem.at[len(copies)])
        copy.start()
        copies.append(copy)

    def turn(part):
        columns = slice(part * width, (part + 1) * width)
        fq_t[columns] = fq[:, columns].T

    def spread_vectors():
        column_at = lax.broadcasted_iota(jnp.int32, (128, width), 1)
        entry = lax.broadcasted_iota(jnp.int32, (128, width), 0)
        spread = jnp.where(lax.rem(column_at, SHARD) == entry, 1.0, 0.0).astype(bf16)
        stacked = jnp.concatenate([gq[p, :16, half_q:] for p in range(DEVICES)], axis=0)
        wide = dot(stacked, spread, 1, 0)
        total = jnp.zeros((16, width), f32)
        column_at = lax.broadcasted_iota(jnp.int32, (16, width), 1)
        for p in range(DEVICES):
            first = SHARD * ((p % CHIPS) * 2 + p // CHIPS)
            here = (column_at >= first) & (column_at < first + SHARD)
            total = total + jnp.where(here, wide[16 * p : 16 * p + 16], 0.0)
        vec_ref[...] = total
        bias[:width] = jnp.broadcast_to(total[2:3], (128, width)).T
        bias[width : 2 * width] = jnp.zeros((width, 128), f32)
        bias[2 * width :] = jnp.broadcast_to(total[3:4], (128, width)).T

    def qkv_part(m, part):
        normed = (unit[m * block : (m + 1) * block] * vec_ref[0:1] + vec_ref[1:2]).astype(bf16)
        lines = slice(part * width, (part + 1) * width)
        result = dot(fq_t[lines], normed, 1, 1)
        added = jnp.concatenate([bias[lines]] * (block // 128), axis=1)
        qkv[m, lines] = (result + added).astype(bf16)
        if part == 2:
            out(qkv.at[m], qkv_hbm.at[m])

    norm_step(0)
    norm_step(1)
    at.await_all()
    own_column(0)
    own_plane(4)
    own_column(1)
    own_plane(2)
    norm_step(2)
    own_plane(3)
    norm_step(3)
    own_plane(1)
    own_column(2)
    own_plane(0)
    own_column(3)
    column(0, 3)
    column(0, 1)
    own_column(4)
    plane(1, 0)
    column(0, 2)
    plane(0, 3)
    column(1, 3)
    plane(0, 1)
    norm_step(4)
    plane(0, 0)
    norm_step(5)
    column(1, 2)
    column(1, 1)
    plane(1, 3)
    plane(0, 2)
    column(2, 3)
    column(2, 1)
    column(2, 2)
    corner(0)
    plane(2, 0)
    plane(2, 3)
    plane(1, 1)
    plane(2, 1)
    plane(1, 2)
    plane(2, 2)
    norm_step(6)
    norm_step(7)
    column(3, 2)
    corner(1)
    plane(4, 0)
    corner(2)
    column(3, 3)
    plane(3, 0)
    others(0)
    others(1)
    column(3, 1)
    others(2)
    column(4, 3)
    build_q()
    column(4, 2)
    turn(0)
    turn(1)
    turn(2)
    spread_vectors()
    column(4, 1)
    qkv_part(0, 0)
    plane(3, 2)
    qkv_part(0, 1)
    qkv_part(0, 2)
    qkv_part(1, 0)
    qkv_part(1, 1)
    qkv_part(1, 2)
    qkv_part(2, 0)
    plane(3, 3)
    plane(4, 2)
    qkv_part(2, 1)
    plane(3, 1)
    plane(4, 3)
    plane(4, 1)
    qkv_part(2, 2)
    qkv_part(3, 0)
    qkv_part(3, 1)
    qkv_part(3, 2)
    qkv_part(4, 0)
    qkv_part(4, 1)
    qkv_part(4, 2)
    qkv_part(5, 0)
    corner(3)
    qkv_part(5, 1)
    qkv_part(5, 2)
    qkv_part(6, 0)
    corner(4)
    qkv_part(6, 1)
    qkv_part(6, 2)
    qkv_part(7, 0)
    others(3)
    qkv_part(7, 1)
    others(4)
    qkv_part(7, 2)
    build_r()
    out(unit_t, unit_hbm)
    for k in range(len(slabs)):
        remote(k, 0, at.sib, 0, DEVICES - 1).wait_send()
    for copy in copies:
        copy.wait()


def gather_and_project(small, w_qkv, w_out, w_in, w_back, tokens, slots):
    rows, width = tokens.shape
    block = rows // slots
    wide = 3 * width
    vmem = pl.BlockSpec(memory_space=pltpu.VMEM)
    anywhere = pl.BlockSpec(memory_space=pl.ANY)
    square = (width, width)
    return pl.pallas_call(
        gather_kernel,
        out_shape=[
            jax.ShapeDtypeStruct((slots, wide, block), bf16),
            jax.ShapeDtypeStruct((width, rows), bf16),
            jax.ShapeDtypeStruct((width, wide), bf16),
            jax.ShapeDtypeStruct(square, bf16),
            jax.ShapeDtypeStruct(square, bf16),
            jax.ShapeDtypeStruct(square, bf16),
            jax.ShapeDtypeStruct((16, width), f32),
        ],
        in_specs=[vmem] * 6,
        out_specs=[anywhere] * 6 + [vmem],
        scratch_shapes=[
            pltpu.VMEM((DEVICES, 2 * SHARD, wide // 2 + 128), bf16),
            pltpu.VMEM((DEVICES, 2 * SHARD, wide // 2), bf16),
            pltpu.VMEM((width, wide), bf16),
            pltpu.VMEM(square, bf16),
            pltpu.VMEM(square, bf16),
            pltpu.VMEM(square, bf16),
            pltpu.VMEM((wide, width), bf16),
            pltpu.VMEM((rows, width), f32),
            pltpu.VMEM((width, rows), bf16),
            pltpu.VMEM((slots, wide, block), bf16),
            pltpu.VMEM((wide, 128), f32),
            pltpu.SemaphoreType.DMA((5,)),
            pltpu.SemaphoreType.DMA((5, CHIPS + 1)),
            pltpu.SemaphoreType.DMA((slots + 5,)),
        ],
        compiler_params=pltpu.CompilerParams(
            collective_id=0, has_side_effects=True, vmem_limit_bytes=58 * MIB
        ),
    )(small, w_qkv, w_out, w_in, w_back, tokens)


def middle_kernel(
    packed,
    head_dim,
    len_ref,
    qkv_ref,
    tok_ref,
    cot_ref,
    wout_ref,
    win_ref,
    wback_ref,
    vec_ref,
    mixed_ref,
    dmix_ref,
    dqkv_ref,
    gvec_ref,
    *rest,
):
    if packed:
        packed_ref, gout_ref, gin_ref, gback_ref, probs, ctx_s, linv_s, dctx_s = rest
    else:
        gout_ref, gin_ref, gback_ref, probs, ctx_s, linv_s, dctx_s = rest
    step = pl.program_id(0)
    block, width = tok_ref.shape
    slot = 32
    group = 4
    heads = width // head_dim
    span = group * head_dim
    scale = head_dim ** (-0.5)
    length = len_ref[step]

    @pl.when(step == 0)
    def _():
        gout_ref[...] = jnp.zeros_like(gout_ref)
        gin_ref[...] = jnp.zeros_like(gin_ref)
        gback_ref[...] = jnp.zeros_like(gback_ref)
        gvec_ref[...] = jnp.zeros_like(gvec_ref)

    def run(size):
        extra = (slot - head_dim, size)
        sub = lax.broadcasted_iota(jnp.int32, extra, 0)
        lane = lax.broadcasted_iota(jnp.int32, extra, 1)
        one_row = jnp.where(sub == 0, 1.0, 0.0).astype(f32)
        two_rows = jnp.where(sub <= 1, 1.0, 0.0).astype(f32)
        mask_row = jnp.where((sub == 0) & (lane >= length), masked_score, 0.0).astype(f32)

        def group_rows(base, g):
            return slice(base + g * span, base + (g + 1) * span)

        def load(base, g):
            return qkv_ref[group_rows(base, g), :size].astype(f32)

        def place(j, rows):
            parts = []
            if j > 0:
                parts.append(jnp.zeros((slot * j, size), bf16))
            parts.append(rows)
            if j < group - 1:
                parts.append(jnp.zeros((slot * (group - 1 - j), size), bf16))
            return jnp.concatenate(parts, axis=0)

        def pieces(values):
            return [values[head_dim * j : head_dim * (j + 1)] for j in range(group)]

        def padded(values, tail):
            return [jnp.concatenate([p, tail], axis=0).astype(bf16) for p in pieces(values)]

        ahead = 3 if size > 128 else 6

        def forward():
            q, k, v, scores, weights, outs = {}, {}, {}, {}, {}, {}
            for t in range(heads + 2 * ahead):
                if t < heads:
                    g, j = divmod(t, group)
                    if j == 0:
                        q[g] = padded(load(0, g), one_row)
                        k[g] = jnp.concatenate(padded(load(width, g), mask_row), axis=0).T
                        v[g] = padded(load(2 * width, g), one_row)
                    scores[t] = dot(k[g], place(j, q[g][j]), 1, 0)
                h = t - ahead
                if 0 <= h < heads:
                    s = scores.pop(h)
                    peak = jnp.max(s, axis=0, keepdims=True)
                    weights[h] = jnp.exp2((s - peak) * (scale * log2_e)).astype(bf16)
                    probs[h, :size, :size] = weights[h]
                h = t - 2 * ahead
                if 0 <= h < heads:
                    g, j = divmod(h, group)
                    o = dot(v[g][j], weights.pop(h), 1, 0)
                    inverse = 1.0 / o[head_dim : head_dim + 1]
                    linv_s[h, :, :size] = jnp.broadcast_to(inverse, (8, size))
                    outs[h] = o[:head_dim] * inverse
                    if j == group - 1:
                        parts = [outs.pop(h - group + 1 + i) for i in range(group)]
                        ctx_s[group_rows(0, g), :size] = jnp.concatenate(parts, axis=0)

        forward()

        live = (lax.broadcasted_iota(jnp.int32, (size, 1), 0) < length).astype(f32)
        out_bias, gain, shift = vec_ref[4:5], vec_ref[5:6], vec_ref[6:7]
        in_bias, back_bias = vec_ref[7:8], vec_ref[8:9]
        x = tok_ref[:size].astype(f32)
        dy = cot_ref[:size].astype(f32)
        ctx_t = ctx_s[:, :size].astype(bf16)
        attn = dot(ctx_t.T, wout_ref[...], 1, 0) + out_bias
        mixed = x + live * attn
        unit, factor = normalize(mixed)
        normed = (unit * gain + shift).astype(bf16)
        pre = dot(normed, win_ref[...], 1, 0) + in_bias
        cdf = 0.5 * (1.0 + lax.erf(pre * 0.7071067811865476))
        act = (pre * cdf).astype(bf16)
        slope = cdf + pre * jnp.exp(-0.5 * pre * pre) * 0.3989422804014327
        branch = dot(act, wback_ref[...], 1, 0) + back_bias
        mixed_ref[:size] = (mixed + live * branch).astype(bf16)
        d_ffn = live * dy
        gvec_ref[4] += fold_rows(d_ffn)
        d_ffn = d_ffn.astype(bf16)
        gback_ref[...] += dot(act.T, d_ffn, 1, 0)
        d_act = dot(d_ffn, wback_ref[...], 1, 1)
        d_pre = (d_act * slope).astype(bf16)
        gvec_ref[3] += fold_rows(d_pre.astype(f32))
        gin_ref[...] += dot(normed.T, d_pre, 1, 0)
        d_normed = dot(d_pre, win_ref[...], 1, 1)
        gvec_ref[1] += fold_rows(d_normed * unit)
        gvec_ref[2] += fold_rows(d_normed)
        d_mixed = dy + norm_backward(d_normed, gain, unit, factor)
        dmix_ref[:size] = d_mixed
        d_attn = (live * d_mixed).astype(bf16)
        gvec_ref[0] += fold_rows(d_attn.astype(f32))
        gout_ref[...] += dot(ctx_t, d_attn, 1, 0)
        dctx_s[:, :size] = dot(wout_ref[...], d_attn, 1, 1).astype(bf16)

        behind = 3 if size > 128 else 6

        def backward():
            q, k, v, d, d_probs, d_scores = {}, {}, {}, {}, {}, {}
            d_q, d_k, d_v = {}, {}, {}
            for t in range(heads + 2 * behind):
                if t < heads:
                    g, j = divmod(t, group)
                    if j == 0:
                        q[g] = padded(load(0, g), one_row)
                        k[g] = padded(load(width, g), one_row)
                        v[g] = jnp.concatenate(padded(load(2 * width, g), two_rows), axis=0).T
                        d_out = pieces(dctx_s[group_rows(0, g), :size].astype(f32))
                        out = pieces(ctx_s[group_rows(0, g), :size])
                        for i in range(group):
                            here = d_out[i] * linv_s[g * group + i, :1, :size]
                            inner = -jnp.sum(here * out[i], axis=0, keepdims=True)
                            high = inner.astype(bf16).astype(f32)
                            blank = jnp.zeros((slot - head_dim - 2, size), f32)
                            tail = [here, high, inner - high, blank]
                            d[g * group + i] = jnp.concatenate(tail, axis=0).astype(bf16)
                    d_probs[t] = dot(v[g], place(j, d[t]), 1, 0)
                h = t - behind
                if 0 <= h < heads:
                    p = probs[h, :size, :size]
                    d_scores[h] = (p.astype(f32) * d_probs.pop(h)).astype(bf16)
                h = t - 2 * behind
                if 0 <= h < heads:
                    g, j = divmod(h, group)
                    ds = d_scores.pop(h)
                    d_v[h] = dot(d.pop(h), probs[h, :size, :size], 1, 1)[:head_dim]
                    d_q[h] = dot(k[g][j], ds, 1, 0)[:head_dim] * scale
                    d_k[h] = dot(q[g][j], ds, 1, 1)[:head_dim] * scale
                    if j == group - 1:
                        for base, parts in ((0, d_q), (width, d_k), (2 * width, d_v)):
                            some = [parts.pop(h - group + 1 + i) for i in range(group)]
                            dqkv_ref[group_rows(base, g), :size] = jnp.concatenate(
                                some, axis=0
                            ).astype(bf16)

        backward()

        if size < block:
            mixed_ref[size:] = tok_ref[size:]
            dmix_ref[size:] = cot_ref[size:].astype(f32)
            dqkv_ref[:, size:] = jnp.zeros((3 * width, block - size), bf16)

    half = block // 2

    @pl.when(length == 0)
    def _():
        mixed_ref[...] = tok_ref[...]
        dmix_ref[...] = cot_ref[...].astype(f32)
        dqkv_ref[...] = jnp.zeros_like(dqkv_ref)

    @pl.when((length > 0) & (length <= half))
    def _():
        run(half)

    @pl.when(length > half)
    def _():
        run(block)

    if packed:

        @pl.when(step == pl.num_programs(0) - 1)
        def _():
            columns = width // 2
            for i in range(DEVICES):
                p = (i % 2) * CHIPS + i // 2
                rows = slice(SHARD * i, SHARD * (i + 1))
                top = jnp.concatenate([gout_ref[rows], gback_ref[rows, :columns]], axis=1)
                bottom = jnp.concatenate([gin_ref[rows], gback_ref[rows, columns:]], axis=1)
                packed_ref[p] = jnp.concatenate([top, bottom], axis=0).astype(bf16)


def middle(mol_len, qkv, tokens, cotangent, w_out, w_in, w_back, vectors, packed):
    slots = mol_len.shape[0]
    rows, width = tokens.shape
    block = rows // slots
    square = (width, width)

    def whole(shape):
        return pl.BlockSpec(shape, lambda m, lengths: (0,) * len(shape))

    by_rows = pl.BlockSpec((block, width), lambda m, lengths: (m, 0))
    out_specs = [
        by_rows,
        by_rows,
        pl.BlockSpec((3 * width, block), lambda m, lengths: (0, m)),
        whole((5, 8, width)),
    ]
    out_shape = [
        jax.ShapeDtypeStruct((rows, width), bf16),
        jax.ShapeDtypeStruct((rows, width), f32),
        jax.ShapeDtypeStruct((3 * width, rows), bf16),
        jax.ShapeDtypeStruct((5, 8, width), f32),
    ]
    scratch = [
        pltpu.VMEM((HEADS, block, block), bf16),
        pltpu.VMEM((width, block), f32),
        pltpu.VMEM((HEADS, 8, block), f32),
        pltpu.VMEM((width, block), bf16),
    ]
    if packed:
        shape = (DEVICES, 2 * SHARD, width + width // 2)
        out_specs.append(whole(shape))
        out_shape.append(jax.ShapeDtypeStruct(shape, bf16))
        scratch = [pltpu.VMEM(square, f32)] * 3 + scratch
    else:
        out_specs += [whole(square)] * 3
        out_shape += [jax.ShapeDtypeStruct(square, f32)] * 3
    return pl.pallas_call(
        functools.partial(middle_kernel, packed, width // HEADS),
        grid_spec=pltpu.PrefetchScalarGridSpec(
            num_scalar_prefetch=1,
            grid=(slots,),
            in_specs=[
                pl.BlockSpec((None, 3 * width, block), lambda m, lengths: (m, 0, 0)),
                by_rows,
                by_rows,
                whole(square),
                whole(square),
                whole(square),
                whole((16, width)),
            ],
            out_specs=out_specs,
            scratch_shapes=scratch,
        ),
        out_shape=out_shape,
        compiler_params=pltpu.CompilerParams(vmem_limit_bytes=58 * MIB),
    )(mol_len, qkv, tokens, cotangent, w_out, w_in, w_back, vectors)


def scatter_kernel(
    sr_hbm,
    dqkv_hbm,
    unit_hbm,
    fq_hbm,
    tok_hbm,
    dmix_hbm,
    vec_ref,
    gvec_ref,
    grad_hbm,
    gq_ref,
    gr_ref,
    sq,
    sr,
    rq_sib,
    rr_sib,
    rq,
    rr,
    dqkv,
    unit_t,
    fq,
    tok,
    dmix,
    grad,
    gain_wide,
    shift_wide,
    small_wide,
    sums,
    result,
    send_sem,
    recv_sem,
    copy_sem,
):
    at = Place()
    at.greet()
    rows, width = tok.shape
    wide = 3 * width
    half_q = wide // 2
    slots = 8
    block = rows // slots
    mine, theirs = at.c * CHIPS, (1 - at.c) * CHIPS
    own = at.block(at.c, at.z, at.y, at.x)
    level_rows = 8 * SHARD

    def local(src, dst, i):
        copy = pltpu.make_async_copy(src, dst, copy_sem.at[i])
        copy.start()
        return copy

    sr_in = local(sr_hbm, sr, 0)
    unit_in = local(unit_hbm, unit_t, 1)
    dqkv_in = local(dqkv_hbm, dqkv, 2)
    fq_in = local(fq_hbm, fq, 3)
    tok_in = local(tok_hbm, tok, 4)
    dmix_in = local(dmix_hbm, dmix, 5)

    slabs = (
        (sq, rq_sib, rq, 0, 640),
        (sq, rq_sib, rq, 640, 640),
        (sr, rr_sib, rr, 0, 1152),
    )

    def cut(ref, k, first, count):
        return ref.at[pl.ds(first, count), :, pl.ds(slabs[k][3], slabs[k][4])]

    def piece(ref, k, p):
        _, _, _, column, columns = slabs[k]
        return ref[p, :, column : column + columns].astype(f32)

    def put(k, p, value):
        slab, _, _, column, columns = slabs[k]
        slab[p, :, column : column + columns] = value.astype(bf16)

    def remote(k, src, dst, target, sem):
        return pltpu.make_async_remote_copy(
            src_ref=src,
            dst_ref=dst,
            send_sem=send_sem.at[k],
            recv_sem=recv_sem.at[k, sem],
            device_id=(target,),
            device_id_type=MESH,
        )

    def x_type(j):
        return at.block(at.c, j, at.y, 1 - at.x)

    def y_type(j):
        return at.block(at.c, j, 1 - at.y, at.x)

    def corner_type(j):
        return at.block(at.c, j, 1 - at.y, 1 - at.x)

    def column_type(j):
        return at.block(at.c, j, at.y, at.x)

    def sib_copy(k, j):
        src = cut(slabs[k][0], k, theirs + 4 * j, 4)
        return remote(k, src, cut(slabs[k][1], k, 4 * j, 4), at.sib, j)

    def sib_send(k, j):
        sib_copy(k, j).start()

    def step_copy(k, src, slot, target):
        src = cut(slabs[k][0], k, src, 1)
        return remote(k, src, cut(slabs[k][2], k, slot, 1), target, PLANES + slot)

    def x_send(k, j):
        step_copy(k, x_type(j), 4 + j, at.xn).start()

    def y_send(k, j):
        step_copy(k, y_type(j), 8 + j, at.yn).start()

    def sib_add(k, j):
        sib_copy(k, j).wait_recv()

        def body(i, carry):
            p = mine + 4 * j + i
            put(k, p, piece(slabs[k][0], k, p) + piece(slabs[k][1], k, 4 * j + i))
            return carry

        lax.fori_loop(0, 4, body, 0)
        step_copy(k, corner_type(j), j, at.yn if j % 2 == 0 else at.xn).start()
        (y_send if j % 2 == 0 else x_send)(k, j)

    def corner_add(k, j):
        step_copy(k, own, j, at.sib).wait_recv()
        p = x_type(j) if j % 2 == 0 else y_type(j)
        put(k, p, piece(slabs[k][0], k, p) + piece(slabs[k][2], k, j))
        (x_send if j % 2 == 0 else y_send)(k, j)

    def plane_add(k, j):
        p = column_type(j)
        step_copy(k, own, 4 + j, at.sib).wait_recv()
        step_copy(k, own, 8 + j, at.sib).wait_recv()
        received = piece(slabs[k][2], k, 4 + j) + piece(slabs[k][2], k, 8 + j)
        put(k, p, piece(slabs[k][0], k, p) + received)

        @pl.when(at.z != j)
        def _():
            step_copy(k, p, 12 + at.z, at.me + 8 * (j - at.z)).start()

    def land(k):
        total = gq_ref if slabs[k][0] is sq else gr_ref
        columns = slice(slabs[k][3], slabs[k][3] + slabs[k][4])
        total[:, columns] = piece(slabs[k][0], k, own)
        for j in range(PLANES):

            @pl.when(at.z != j)
            def _():
                step_copy(k, own, 12 + j, at.sib).wait_recv()
                total[:, columns] += piece(slabs[k][2], k, 12 + j)

    def prepare():
        gain_wide[...] = jnp.broadcast_to(vec_ref[0:1], (128, width)).T
        shift_wide[...] = jnp.broadcast_to(vec_ref[1:2], (128, width)).T
        ones = jnp.ones((16, rows), bf16)
        for part in range(3):
            columns = slice(part * width, (part + 1) * width)
            sums[:, columns] = dot(ones, dqkv[columns], 1, 1)[:8]
        lines = [jnp.zeros((2, width), f32), sums[0:1, :width], sums[0:1, 2 * width :]]
        lines += [jnp.sum(gvec_ref[i], axis=0, keepdims=True) for i in range(5)]
        lines.append(jnp.zeros((128 - 9, width), f32))
        small_wide[...] = jnp.concatenate(lines, axis=0).T

    def weight_grad(j, part):
        lines = pl.ds(j * level_rows, level_rows)
        columns = slice(part * width, (part + 1) * width)
        product = dot(unit_t[lines], dqkv[columns], 1, 1)
        weight = fq[lines, columns].astype(f32)
        line = sums[0:1, columns]
        gain_sum = jnp.sum(weight * product, axis=1, keepdims=True)
        shift_sum = jnp.sum(weight * line, axis=1, keepdims=True)
        lane = lax.broadcasted_iota(jnp.int32, (level_rows, 128), 1)
        small_wide[lines] += jnp.where(
            lane == 0, gain_sum, jnp.where(lane == 1, shift_sum, 0.0)
        )
        gain = jnp.concatenate([gain_wide[lines]] * (width // 128), axis=1)
        shift = jnp.concatenate([shift_wide[lines]] * (width // 128), axis=1)
        result[:, columns] = gain * product + shift * line
        if part < 2:
            return
        small = small_wide[lines]
        blank = jnp.zeros((SHARD, 128), f32)
        for i in range(8):
            p = (i % 2) * CHIPS + 4 * j + i // 2
            some = slice(SHARD * i, SHARD * (i + 1))
            top = jnp.concatenate([result[some, :half_q], small[some]], axis=1)
            bottom = jnp.concatenate([result[some, half_q:], blank], axis=1)
            sq[p] = jnp.concatenate([top, bottom], axis=0).astype(bf16)

    grads = []

    def input_grad(m):
        some = slice(m * block, (m + 1) * block)
        d_normed = dot(fq[...], dqkv[:, some], 1, 0).T
        unit, factor = normalize(tok[some].astype(f32))
        share = norm_backward(d_normed, vec_ref[0:1], unit, factor)
        grad[some] = (dmix[some] + share).astype(bf16)
        grads.append(local(grad.at[pl.ds(m * block, block)], grad_hbm.at[pl.ds(m * block, block)], 6 + m))

    sr_in.wait()
    at.await_all()
    sib_send(2, 0)
    sib_send(2, 1)
    sib_send(2, 2)
    sib_add(2, 0)
    sib_send(2, 3)
    sib_add(2, 1)
    sib_add(2, 2)
    sib_add(2, 3)
    unit_in.wait()
    dqkv_in.wait()
    fq_in.wait()
    prepare()
    weight_grad(0, 0)
    weight_grad(0, 1)
    weight_grad(0, 2)
    weight_grad(3, 0)
    corner_add(2, 1)
    sib_send(1, 0)
    corner_add(2, 0)
    corner_add(2, 3)
    weight_grad(3, 1)
    sib_send(0, 0)
    corner_add(2, 2)
    weight_grad(3, 2)
    sib_send(1, 3)
    sib_send(0, 3)
    sib_add(0, 0)
    sib_add(1, 0)
    weight_grad(2, 0)
    plane_add(2, 1)
    plane_add(2, 0)
    sib_add(1, 3)
    weight_grad(2, 1)
    sib_add(0, 3)
    plane_add(2, 3)
    weight_grad(2, 2)
    sib_send(1, 2)
    weight_grad(1, 0)
    sib_add(1, 2)
    corner_add(0, 0)
    plane_add(2, 2)
    sib_send(0, 2)
    corner_add(1, 0)
    weight_grad(1, 1)
    corner_add(0, 3)
    weight_grad(1, 2)
    sib_send(1, 1)
    sib_send(0, 1)
    corner_add(1, 2)
    plane_add(0, 0)
    tok_in.wait()
    dmix_in.wait()
    sib_add(0, 2)
    corner_add(1, 3)
    sib_add(1, 1)
    sib_add(0, 1)
    plane_add(0, 3)
    plane_add(1, 0)
    input_grad(0)
    plane_add(1, 2)
    corner_add(0, 2)
    corner_add(1, 1)
    input_grad(1)
    input_grad(2)
    corner_add(0, 1)
    plane_add(1, 3)
    plane_add(1, 1)
    input_grad(3)
    input_grad(4)
    plane_add(0, 2)
    plane_add(0, 1)
    input_grad(5)
    input_grad(6)
    land(1)
    input_grad(7)
    land(2)
    land(0)
    for k in range(len(slabs)):
        every = cut(slabs[k][0], k, 0, DEVICES - 1)
        remote(k, every, every, at.sib, 0).wait_send()
    for copy in grads:
        copy.wait()


def scatter(packed, dqkv, unit_t, full_qkv, tokens, d_mixed, vectors, sums):
    rows, width = tokens.shape
    wide = 3 * width
    vmem = pl.BlockSpec(memory_space=pltpu.VMEM)
    anywhere = pl.BlockSpec(memory_space=pl.ANY)
    tall = 2 * SHARD
    widths = (wide // 2 + 128, wide // 2)
    return pl.pallas_call(
        scatter_kernel,
        out_shape=[jax.ShapeDtypeStruct((rows, width), bf16)]
        + [jax.ShapeDtypeStruct((tall, w), f32) for w in widths],
        in_specs=[anywhere] * 6 + [vmem] * 2,
        out_specs=[anywhere] + [vmem] * 2,
        scratch_shapes=[pltpu.VMEM((DEVICES, tall, w), bf16) for w in widths]
        + [pltpu.VMEM((CHIPS, tall, w), bf16) for w in widths]
        + [pltpu.VMEM((4 * PLANES, tall, w), bf16) for w in widths]
        + [
            pltpu.VMEM((wide, rows), bf16),
            pltpu.VMEM((width, rows), bf16),
            pltpu.VMEM((width, wide), bf16),
            pltpu.VMEM((rows, width), bf16),
            pltpu.VMEM((rows, width), f32),
            pltpu.VMEM((rows, width), bf16),
            pltpu.VMEM((width, 128), f32),
            pltpu.VMEM((width, 128), f32),
            pltpu.VMEM((width, 128), f32),
            pltpu.VMEM((8, wide), f32),
            pltpu.VMEM((8 * SHARD, wide), f32),
            pltpu.SemaphoreType.DMA((3,)),
            pltpu.SemaphoreType.DMA((3, 5 * PLANES)),
            pltpu.SemaphoreType.DMA((14,)),
        ],
        compiler_params=pltpu.CompilerParams(
            collective_id=1, has_side_effects=True, vmem_limit_bytes=60 * MIB
        ),
    )(packed, dqkv, unit_t, full_qkv, tokens, d_mixed, vectors, sums)


def finish_kernel(grad_ref, q_ref, r_ref, out_ref, g_qkv, g_out, g_in, g_back, *lines):
    out_ref[...] = grad_ref[...]

    @pl.when(pl.program_id(0) == 0)
    def _():
        width = g_out.shape[1]
        half_q = 3 * width // 2
        half = width // 2
        g_qkv[:, :half_q] = q_ref[:SHARD, :half_q]
        g_qkv[:, half_q:] = q_ref[SHARD:, :half_q]
        g_out[...] = r_ref[:SHARD, :width]
        g_in[...] = r_ref[SHARD:, :width]
        g_back[:, :half] = r_ref[:SHARD, width:]
        g_back[:, half:] = r_ref[SHARD:, width:]
        small = q_ref[:SHARD, half_q:].T
        for i, line in enumerate(lines):
            line[...] = small[i, :SHARD]


def finish(token_grad, q_part, r_part):
    rows, width = token_grad.shape
    pieces = 4
    by_rows = pl.BlockSpec((rows // pieces, width), lambda i: (i, 0))

    def whole(shape):
        return pl.BlockSpec(shape, lambda i: (0,) * len(shape))

    shapes = [(SHARD, 3 * width)] + [(SHARD, width)] * 3 + [(SHARD,)] * 9
    return pl.pallas_call(
        finish_kernel,
        grid=(pieces,),
        out_shape=[jax.ShapeDtypeStruct(token_grad.shape, bf16)]
        + [jax.ShapeDtypeStruct(s, f32) for s in shapes],
        in_specs=[by_rows, whole(q_part.shape), whole(r_part.shape)],
        out_specs=[by_rows] + [whole(s) for s in shapes],
    )(token_grad, q_part, r_part)


def on_one_plan(tokens, mol_len, cotangent, vectors, w_qkv, w_out, w_in, w_back):
    slots = mol_len.shape[0]
    small = jnp.pad(jnp.stack(vectors), ((0, 16 - len(vectors)), (0, 128 - SHARD)))
    qkv, unit_t, full_qkv, full_out, full_in, full_back, lines = gather_and_project(
        small, w_qkv, w_out, w_in, w_back, tokens, slots
    )
    mixed_out, d_mixed, dqkv, sums, packed = middle(
        mol_len, qkv, tokens, cotangent, full_out, full_in, full_back, lines, True
    )
    token_grad, q_part, r_part = scatter(
        packed, dqkv, unit_t, full_qkv, tokens, d_mixed, lines, sums
    )
    token_grad, g_qkv, g_out, g_in, g_back, *small = finish(token_grad, q_part, r_part)
    return mixed_out, token_grad, small, g_qkv, g_out, g_in, g_back


def on_any_plan(tokens, mol_len, cotangent, vectors, w_qkv, w_out, w_in, w_back):
    slots = mol_len.shape[0]
    rows, width = tokens.shape

    def gather(array, axis):
        return lax.all_gather(array, "fsdp", axis=axis, tiled=True)

    lines = gather(jnp.stack(vectors), 1).astype(f32)
    lines = jnp.pad(lines, ((0, 16 - len(vectors)), (0, 0)))
    full_qkv, full_out, full_in, full_back = (
        gather(w, 0) for w in (w_qkv, w_out, w_in, w_back)
    )
    unit, factor = normalize(tokens.astype(f32))
    normed = (unit * lines[0] + lines[1]).astype(bf16)
    qkv = jnp.dot(normed, full_qkv, preferred_element_type=f32)
    qkv = (qkv + jnp.concatenate([lines[2], jnp.zeros_like(lines[2]), lines[3]])).astype(bf16)
    qkv = qkv.reshape(slots, rows // slots, 3 * width).transpose(0, 2, 1)
    mixed_out, d_mixed, dqkv, sums, g_out, g_in, g_back = middle(
        mol_len, qkv, tokens, cotangent, full_out, full_in, full_back, lines, False
    )
    g_qkv = jnp.einsum("rf,dr->fd", normed, dqkv, preferred_element_type=f32)
    d_normed = jnp.einsum("dr,fd->rf", dqkv, full_qkv, preferred_element_type=f32)
    totals = jnp.sum(dqkv.astype(f32), axis=1)
    small = [jnp.sum(d_normed * unit, axis=0), jnp.sum(d_normed, axis=0)]
    small += [totals[:width], totals[2 * width :]]
    small += [jnp.sum(sums[i], axis=0) for i in range(5)]
    share = norm_backward(d_normed, lines[0], unit, factor)
    token_grad = (d_mixed + share).astype(bf16)

    def scatter_sum(array, axis):
        return lax.psum_scatter(array, "fsdp", scatter_dimension=axis, tiled=True)

    small = scatter_sum(jnp.stack(small), 1)
    return (
        mixed_out,
        token_grad,
        [small[i] for i in range(9)],
        *(scatter_sum(g, 0) for g in (g_qkv, g_out, g_in, g_back)),
    )


def per_device(
    devices,
    tokens,
    mol_len,
    cotangent,
    ln1_gain,
    ln1_bias,
    w_qkv,
    q_bias,
    v_bias,
    w_out,
    out_bias,
    ln2_gain,
    ln2_bias,
    w_in,
    in_bias,
    w_back,
    back_bias,
):
    vectors = [
        ln1_gain,
        ln1_bias,
        q_bias,
        v_bias,
        out_bias,
        ln2_gain,
        ln2_bias,
        in_bias,
        back_bias,
    ]
    known = devices == DEVICES and w_qkv.shape[0] == SHARD
    plan = on_one_plan if known else on_any_plan
    mixed_out, token_grad, small, g_qkv, g_out, g_in, g_back = plan(
        tokens, mol_len, cotangent, vectors, w_qkv, w_out, w_in, w_back
    )
    return (
        mixed_out,
        token_grad,
        small[0],
        small[1],
        g_qkv,
        small[2],
        small[3],
        g_out,
        small[4],
        small[5],
        small[6],
        g_in,
        small[7],
        g_back,
        small[8],
    )


def solution(mesh):
    line, matrix = P("fsdp"), P("fsdp", None)
    return jax.shard_map(
        functools.partial(per_device, mesh.shape["fsdp"]),
        mesh=mesh,
        in_specs=(
            matrix,
            line,
            matrix,
            line,
            line,
            matrix,
            line,
            line,
            matrix,
            line,
            line,
            line,
            matrix,
            line,
            matrix,
            line,
        ),
        out_specs=(
            matrix,
            matrix,
            line,
            line,
            matrix,
            line,
            line,
            matrix,
            line,
            line,
            line,
            matrix,
            line,
            matrix,
            line,
        ),
        check_vma=False,
    )
```

time: 248 us -> 199 us (0.80); the launches traced: 247 us -> 200 us
  Pallas kernels: 235 us -> 197 us
  local copies, waits for them, and re-layouts: 10.4 us -> 2.07 us
    pallas_call x1, Pallas kernels: 115 us -> 50.7 us  [scatter(): pl.pallas_call(scatter_kernel, out_shape=[jax.ShapeDtypeStruct((rows, wid...]
    pallas_call x1, Pallas kernels: 53.2 us -> 75.6 us  [middle(): pl.pallas_call(functools.partial(middle_kernel, packed, width // HEADS),...]
    unnamed x13 -> x0, local copies, waits for them, and re-layouts: 6.41 us -> none
    pallas_call x0 -> x1, Pallas kernels: none -> 4.59 us  [finish(): pl.pallas_call(finish_kernel, grid=(pieces,), out_shape=[jax.ShapeDtypeSt...]
where the time goes in v2:
time: 199 us; the launch traced here: 200 us
  Pallas kernels  197 us (99%)
  local copies, waits for them, and re-layouts  2.07 us (1%)
    pallas_call x1, Pallas kernels, middle(): pl.pallas_call(functools.partial(middle_kernel, packed, width // HEADS),...  75.6 us
    pallas_call x1, Pallas kernels, gather_and_project(): pl.pallas_call(gather_kernel, out_shape=[jax.ShapeDtypeStruct((slots, wid...  66.5 us
    pallas_call x1, Pallas kernels, scatter(): pl.pallas_call(scatter_kernel, out_shape=[jax.ShapeDtypeStruct((rows, wid...  50.7 us
    pallas_call x1, Pallas kernels, finish(): pl.pallas_call(finish_kernel, grid=(pieces,), out_shape=[jax.ShapeDtypeSt...  4.59 us

profile of v2, /device:TPU:0, one launch (start us, length us, event | category | flops | bytes accessed | tf_op | source)
XLA Modules:
  0.0 200.5 jit_solution(14416870716405532818)
XLA Ops:
  0.6 1.5 stack.39
  2.1 0.6 pad.4.small_ref
  2.7 66.5 %shard_map.271 = (bf16[8,2304,256]{2,1,0:T(8,128)(2,1)}, bf16[768,2048]{1,0:T(8,128)(2,1)}, bf16[768,2304]{1,0:T(8,128)(2,1)}, bf16[768,768]{1,0:T(8,128)(2,1)},...) custom-call(bf16[16,128]{1,0:T(8,128)(2,1)} %pad.4.small_ref, bf16[24,2304]{1,0:T(8,128)(2,1)} %wq_ref.1, ...), custom_call_target="tpu_custom_call" | custom-call | tf_op jit(solution)/shard_map/pallas_call | solution.py:394
  69.2 75.6 %shard_map.272 = (bf16[2048,768]{1,0:T(8,128)(2,1)}, f32[2048,768]{1,0:T(8,128)}, bf16[2304,2048]{1,0:T(8,128)(2,1)}, f32[5,8,768]{2,1,0:T(8,128)}, bf16[32,48,1152]{2,1,0:T(8,128)(2,1)}) custom-call(s32[8]{0:T(128)} %len_ref.1, bf16[8,2304,256]{2,1,0:T(8,128)(2,1)} %get-tuple-element.44.qkv_ref, bf16[2048,768]{1,0:T(8,128)(2,1)} %tok_hbm.1, ...), custom_call_target="tpu_custom_call" | custom-call | tf_op jit(solution)/shard_map/pallas_call | solution.py:672
  144.9 50.7 %shard_map.273 = (bf16[2048,768]{1,0:T(8,128)(2,1)}, f32[48,1280]{1,0:T(8,128)}, f32[48,1152]{1,0:T(8,128)}) custom-call(bf16[32,48,1152]{2,1,0:T(8,128)(2,1)} %get-tuple-element.50.sr_hbm, bf16[2304,2048]{1,0:T(8,128)(2,1)} %get-tuple-element.51.dqkv_hbm, bf16[768,2048]{1,0:T(8,128)(2,1)} %get-tuple-element.52.unit_hbm, ...), custom_call_target="tpu_custom_call" | custom-call | tf_op jit(solution)/shard_map/pallas_call | solution.py:987
  195.6 4.6 %shard_map.274 = (bf16[2048,768]{1,0:T(8,128)(2,1)}, f32[24,2304]{1,0:T(8,128)}, f32[24,768]{1,0:T(8,128)}, f32[24,768]{1,0:T(8,128)}, f32[24,768]{1,0:T(8,128)}...) custom-call(bf16[2048,768]{1,0:T(8,128)(2,1)} %get-tuple-element.56., ...), custom_call_target="tpu_custom_call" | custom-call | tf_op jit(solution)/shard_map/pallas_call | solution.py:1046

commit v3 on v2

--- a/solution.py
+++ b/solution.py
@@ -77,19 +77,24 @@
 
 
 def gather_kernel(
+    len_ref,
     small_ref,
     wq_ref,
     wo_ref,
     wi_ref,
     wb_ref,
     tok_ref,
+    cot_hbm,
     qkv_hbm,
     unit_hbm,
     fq_hbm,
     fo_hbm,
     fi_hbm,
     fb_hbm,
+    tok_hbm,
+    cot_out,
     vec_ref,
+    work_ref,
     gq,
     gr,
     fq,
@@ -101,14 +106,21 @@
     unit_t,
     qkv,
     bias,
+    tok_odd,
+    cot_odd,
+    len_send,
+    len_recv,
     send_sem,
     recv_sem,
+    swap_send,
+    swap_recv,
     copy_sem,
 ):
     at = Place()
     at.greet()
     width = tok_ref.shape[1]
     slots, _, block = qkv.shape
+    shared = slots // 2
     half_q = 3 * width // 2
     half = width // 2
     own = at.block(at.c, at.z, at.y, at.x)
@@ -208,9 +220,63 @@
     def others(k):
         remote(k, theirs, at.sib, CHIPS, CHIPS).wait_recv()
 
+    def rows_of(i):
+        return pl.ds(i * block, block)
+
+    cot_in = [
+        pltpu.make_async_copy(
+            cot_hbm.at[rows_of(2 * i + 1)], cot_odd.at[rows_of(i)], swap_recv.at[6 + i]
+        )
+        for i in range(shared)
+    ]
+
+    def swap_copy(src, dst, send, recv):
+        return pltpu.make_async_remote_copy(
+            src_ref=src,
+            dst_ref=dst,
+            send_sem=swap_send.at[send],
+            recv_sem=swap_recv.at[recv],
+            device_id=(at.sib,),
+            device_id_type=MESH,
+        )
+
+    def tok_copy(i):
+        return swap_copy(tok_ref.at[rows_of(2 * i + 1)], tok_odd.at[rows_of(i)], 0, i)
+
+    def swap_start():
+        swap_copy(len_send, len_recv, 2, 5).start()
+        for i in range(shared):
+            tok_copy(i).start()
+        for i in range(shared):
+            cot_in[i].wait()
+            swap_copy(cot_odd.at[rows_of(i)], cot_out.at[rows_of(i)], 1, 4).start()
+
+    def swap_end():
+        swap_copy(len_send, len_recv, 2, 5).wait()
+        swap_copy(tok_odd, tok_odd, 0, 0).wait_send()
+        swap_copy(cot_odd, cot_out, 1, 4).wait()
+        place = lax.broadcasted_iota(jnp.int32, (shared, 128), 0)
+        own_lengths = jnp.zeros((shared, 128), jnp.int32)
+        odd_lengths = jnp.zeros((shared, 128), jnp.int32)
+        for i in range(shared):
+            own_lengths = jnp.where(place == i, len_send[2 * i : 2 * i + 1], own_lengths)
+            odd_lengths = jnp.where(place == i, len_recv[2 * i + 1 : 2 * i + 2], odd_lengths)
+        work_ref[:shared] = own_lengths
+        work_ref[shared:] = odd_lengths
+
+    for i in range(slots):
+        len_send[i : i + 1] = jnp.full((1, 128), len_ref[i], jnp.int32)
+    for copy in cot_in:
+        copy.start()
+
     def norm_step(m):
-        rows = pl.ds(m * block, block)
-        values, _ = normalize(tok_ref[rows].astype(f32))
+        rows = rows_of(m)
+        if m < shared:
+            here = tok_ref[rows_of(2 * m)]
+        else:
+            tok_copy(m - shared).wait_recv()
+            here = tok_odd[rows_of(m - shared)]
+        values, _ = normalize(here.astype(f32))
         unit[rows] = values
         unit_t[:, rows] = values.astype(bf16).T
 
@@ -286,6 +352,7 @@
     norm_step(0)
     norm_step(1)
     at.await_all()
+    swap_start()
     own_column(0)
     own_plane(4)
     own_column(1)
@@ -378,13 +445,16 @@
     qkv_part(7, 2)
     build_r()
     out(unit_t, unit_hbm)
+    out(tok_odd, tok_hbm)
+    swap_end()
     for k in range(len(slabs)):
         remote(k, 0, at.sib, 0, DEVICES - 1).wait_send()
     for copy in copies:
         copy.wait()
 
 
-def gather_and_project(small, w_qkv, w_out, w_in, w_back, tokens, slots):
+def gather_and_project(mol_len, small, w_qkv, w_out, w_in, w_back, tokens, cotangent):
+    slots = mol_len.shape[0]
     rows, width = tokens.shape
     block = rows // slots
     wide = 3 * width
@@ -400,10 +470,13 @@
             jax.ShapeDtypeStruct(square, bf16),
             jax.ShapeDtypeStruct(square, bf16),
             jax.ShapeDtypeStruct(square, bf16),
+            jax.ShapeDtypeStruct((rows // 2, width), bf16),
+            jax.ShapeDtypeStruct((rows // 2, width), bf16),
             jax.ShapeDtypeStruct((16, width), f32),
+            jax.ShapeDtypeStruct((slots, 128), jnp.int32),
         ],
-        in_specs=[vmem] * 6,
-        out_specs=[anywhere] * 6 + [vmem],
+        in_specs=[pl.BlockSpec(memory_space=pltpu.SMEM)] + [vmem] * 6 + [anywhere],
+        out_specs=[anywhere] * 8 + [vmem] * 2,
         scratch_shapes=[
             pltpu.VMEM((DEVICES, 2 * SHARD, wide // 2 + 128), bf16),
             pltpu.VMEM((DEVICES, 2 * SHARD, wide // 2), bf16),
@@ -416,14 +489,20 @@
             pltpu.VMEM((width, rows), bf16),
             pltpu.VMEM((slots, wide, block), bf16),
             pltpu.VMEM((wide, 128), f32),
+            pltpu.VMEM((rows // 2, width), bf16),
+            pltpu.VMEM((rows // 2, width), bf16),
+            pltpu.VMEM((slots, 128), jnp.int32),
+            pltpu.VMEM((slots, 128), jnp.int32),
             pltpu.SemaphoreType.DMA((5,)),
             pltpu.SemaphoreType.DMA((5, CHIPS + 1)),
-            pltpu.SemaphoreType.DMA((slots + 5,)),
+            pltpu.SemaphoreType.DMA((3,)),
+            pltpu.SemaphoreType.DMA((6 + slots // 2,)),
+            pltpu.SemaphoreType.DMA((slots + 6,)),
         ],
         compiler_params=pltpu.CompilerParams(
-            collective_id=0, has_side_effects=True, vmem_limit_bytes=58 * MIB
+            collective_id=0, has_side_effects=True, vmem_limit_bytes=60 * MIB
         ),
-    )(small, w_qkv, w_out, w_in, w_back, tokens)
+    )(mol_len, small, w_qkv, w_out, w_in, w_back, tokens, cotangent)
 
 
 def middle_kernel(
@@ -431,8 +510,10 @@
     head_dim,
     len_ref,
     qkv_ref,
-    tok_ref,
-    cot_ref,
+    tok_first,
+    tok_second,
+    cot_first,
+    cot_second,
     wout_ref,
     win_ref,
     wback_ref,
@@ -444,9 +525,10 @@
     *rest,
 ):
     if packed:
-        packed_ref, gout_ref, gin_ref, gback_ref, probs, ctx_s, linv_s, dctx_s = rest
+        packed_ref, gout_ref, gin_ref, gback_ref, *rest = rest
     else:
-        gout_ref, gin_ref, gback_ref, probs, ctx_s, linv_s, dctx_s = rest
+        gout_ref, gin_ref, gback_ref, *rest = rest
+    probs, ctx_s, linv_s, dctx_s, tok_ref, cot_ref = rest
     step = pl.program_id(0)
     block, width = tok_ref.shape
     slot = 32
@@ -454,7 +536,10 @@
     heads = width // head_dim
     span = group * head_dim
     scale = head_dim ** (-0.5)
-    length = len_ref[step]
+    length = len_ref[step, 0]
+    first = step < pl.num_programs(0) // 2
+    tok_ref[...] = jnp.where(first, tok_first[...], tok_second[...])
+    cot_ref[...] = jnp.where(first, cot_first[...], cot_second[...])
 
     @pl.when(step == 0)
     def _():
@@ -633,20 +718,26 @@
                 packed_ref[p] = jnp.concatenate([top, bottom], axis=0).astype(bf16)
 
 
-def middle(mol_len, qkv, tokens, cotangent, w_out, w_in, w_back, vectors, packed):
-    slots = mol_len.shape[0]
-    rows, width = tokens.shape
-    block = rows // slots
+def middle(lengths, qkv, tokens, cotangent, w_out, w_in, w_back, vectors, packed):
+    slots, wide, block = qkv.shape
+    rows, width = slots * block, wide // 3
     square = (width, width)
+    shared = slots // 2
 
     def whole(shape):
-        return pl.BlockSpec(shape, lambda m, lengths: (0,) * len(shape))
-
-    by_rows = pl.BlockSpec((block, width), lambda m, lengths: (m, 0))
+        return pl.BlockSpec(shape, lambda m: (0,) * len(shape))
+
+    by_rows = pl.BlockSpec((block, width), lambda m: (m, 0))
+    if packed:
+        first = pl.BlockSpec((block, width), lambda m: (2 * jnp.minimum(m, shared - 1), 0))
+        second = pl.BlockSpec((block, width), lambda m: (jnp.maximum(m - shared, 0), 0))
+    else:
+        first = pl.BlockSpec((block, width), lambda m: (jnp.minimum(m, shared - 1), 0))
+        second = pl.BlockSpec((block, width), lambda m: (jnp.maximum(m, shared), 0))
     out_specs = [
         by_rows,
         by_rows,
-        pl.BlockSpec((3 * width, block), lambda m, lengths: (0, m)),
+        pl.BlockSpec((3 * width, block), lambda m: (0, m)),
         whole((5, 8, width)),
     ]
     out_shape = [
@@ -660,6 +751,8 @@
         pltpu.VMEM((width, block), f32),
         pltpu.VMEM((HEADS, 8, block), f32),
         pltpu.VMEM((width, block), bf16),
+        pltpu.VMEM((block, width), bf16),
+        pltpu.VMEM((block, width), bf16),
     ]
     if packed:
         shape = (DEVICES, 2 * SHARD, width + width // 2)
@@ -671,24 +764,24 @@
         out_shape += [jax.ShapeDtypeStruct(square, f32)] * 3
     return pl.pallas_call(
         functools.partial(middle_kernel, packed, width // HEADS),
-        grid_spec=pltpu.PrefetchScalarGridSpec(
-            num_scalar_prefetch=1,
-            grid=(slots,),
-            in_specs=[
-                pl.BlockSpec((None, 3 * width, block), lambda m, lengths: (m, 0, 0)),
-                by_rows,
-                by_rows,
-                whole(square),
-                whole(square),
-                whole(square),
-                whole((16, width)),
-            ],
-            out_specs=out_specs,
-            scratch_shapes=scratch,
-        ),
+        grid=(slots,),
+        in_specs=[
+            pl.BlockSpec(memory_space=pltpu.SMEM),
+            pl.BlockSpec((None, 3 * width, block), lambda m: (m, 0, 0)),
+            first,
+            second,
+            first,
+            second,
+            whole(square),
+            whole(square),
+            whole(square),
+            whole((16, width)),
+        ],
+        out_specs=out_specs,
+        scratch_shapes=scratch,
         out_shape=out_shape,
         compiler_params=pltpu.CompilerParams(vmem_limit_bytes=58 * MIB),
-    )(mol_len, qkv, tokens, cotangent, w_out, w_in, w_back, vectors)
+    )(lengths, qkv, *tokens, *cotangent, w_out, w_in, w_back, vectors)
 
 
 def scatter_kernel(
@@ -697,10 +790,14 @@
     unit_hbm,
     fq_hbm,
     tok_hbm,
+    odd_hbm,
     dmix_hbm,
+    mixed_hbm,
     vec_ref,
     gvec_ref,
     grad_hbm,
+    grad_out,
+    mixed_out,
     gq_ref,
     gr_ref,
     sq,
@@ -715,6 +812,7 @@
     tok,
     dmix,
     grad,
+    mixed,
     gain_wide,
     shift_wide,
     small_wide,
@@ -722,6 +820,8 @@
     result,
     send_sem,
     recv_sem,
+    swap_send,
+    swap_recv,
     copy_sem,
 ):
     at = Place()
@@ -744,8 +844,25 @@
     unit_in = local(unit_hbm, unit_t, 1)
     dqkv_in = local(dqkv_hbm, dqkv, 2)
     fq_in = local(fq_hbm, fq, 3)
-    tok_in = local(tok_hbm, tok, 4)
-    dmix_in = local(dmix_hbm, dmix, 5)
+    shared = slots // 2
+
+    def rows_of(i, count=1):
+        return pl.ds(i * block, count * block)
+
+    mixed_in = local(mixed_hbm.at[rows_of(shared, shared)], mixed, 4)
+    late = [local(dmix_hbm, dmix, 5), local(odd_hbm, tok.at[rows_of(shared, shared)], 6)]
+    for i in range(shared):
+        late.append(local(tok_hbm.at[rows_of(2 * i)], tok.at[rows_of(i)], 7 + i))
+
+    def swap_copy(src, dst, i):
+        return pltpu.make_async_remote_copy(
+            src_ref=src,
+            dst_ref=dst,
+            send_sem=swap_send.at[i],
+            recv_sem=swap_recv.at[i],
+            device_id=(at.sib,),
+            device_id_type=MESH,
+        )
 
     slabs = (
         (sq, rq_sib, rq, 0, 640),
@@ -889,7 +1006,10 @@
         unit, factor = normalize(tok[some].astype(f32))
         share = norm_backward(d_normed, vec_ref[0:1], unit, factor)
         grad[some] = (dmix[some] + share).astype(bf16)
-        grads.append(local(grad.at[pl.ds(m * block, block)], grad_hbm.at[pl.ds(m * block, block)], 6 + m))
+        if m < shared:
+            grads.append(local(grad.at[rows_of(m)], grad_hbm.at[rows_of(m)], 7 + shared + m))
+        else:
+            swap_copy(grad.at[rows_of(m)], grad_out.at[rows_of(m - shared)], 0).start()
 
     sr_in.wait()
     at.await_all()
@@ -943,8 +1063,10 @@
     sib_send(0, 1)
     corner_add(1, 2)
     plane_add(0, 0)
-    tok_in.wait()
-    dmix_in.wait()
+    mixed_in.wait()
+    swap_copy(mixed, mixed_out, 1).start()
+    for copy in late:
+        copy.wait()
     sib_add(0, 2)
     corner_add(1, 3)
     sib_add(1, 1)
@@ -975,9 +1097,11 @@
         remote(k, every, every, at.sib, 0).wait_send()
     for copy in grads:
         copy.wait()
-
-
-def scatter(packed, dqkv, unit_t, full_qkv, tokens, d_mixed, vectors, sums):
+    swap_copy(grad.at[rows_of(shared, shared)], grad_out, 0).wait()
+    swap_copy(mixed, mixed_out, 1).wait()
+
+
+def scatter(packed, dqkv, unit_t, full_qkv, tokens, odd_tokens, d_mixed, mixed, vectors, sums):
     rows, width = tokens.shape
     wide = 3 * width
     vmem = pl.BlockSpec(memory_space=pltpu.VMEM)
@@ -986,10 +1110,10 @@
     widths = (wide // 2 + 128, wide // 2)
     return pl.pallas_call(
         scatter_kernel,
-        out_shape=[jax.ShapeDtypeStruct((rows, width), bf16)]
+        out_shape=[jax.ShapeDtypeStruct((rows // 2, width), bf16)] * 3
         + [jax.ShapeDtypeStruct((tall, w), f32) for w in widths],
-        in_specs=[anywhere] * 6 + [vmem] * 2,
-        out_specs=[anywhere] + [vmem] * 2,
+        in_specs=[anywhere] * 8 + [vmem] * 2,
+        out_specs=[anywhere] * 3 + [vmem] * 2,
         scratch_shapes=[pltpu.VMEM((DEVICES, tall, w), bf16) for w in widths]
         + [pltpu.VMEM((CHIPS, tall, w), bf16) for w in widths]
         + [pltpu.VMEM((4 * PLANES, tall, w), bf16) for w in widths]
@@ -1000,6 +1124,7 @@
             pltpu.VMEM((rows, width), bf16),
             pltpu.VMEM((rows, width), f32),
             pltpu.VMEM((rows, width), bf16),
+            pltpu.VMEM((rows // 2, width), bf16),
             pltpu.VMEM((width, 128), f32),
             pltpu.VMEM((width, 128), f32),
             pltpu.VMEM((width, 128), f32),
@@ -1007,16 +1132,24 @@
             pltpu.VMEM((8 * SHARD, wide), f32),
             pltpu.SemaphoreType.DMA((3,)),
             pltpu.SemaphoreType.DMA((3, 5 * PLANES)),
-            pltpu.SemaphoreType.DMA((14,)),
+            pltpu.SemaphoreType.DMA((2,)),
+            pltpu.SemaphoreType.DMA((2,)),
+            pltpu.SemaphoreType.DMA((15,)),
         ],
         compiler_params=pltpu.CompilerParams(
             collective_id=1, has_side_effects=True, vmem_limit_bytes=60 * MIB
         ),
-    )(packed, dqkv, unit_t, full_qkv, tokens, d_mixed, vectors, sums)
-
-
-def finish_kernel(grad_ref, q_ref, r_ref, out_ref, g_qkv, g_out, g_in, g_back, *lines):
-    out_ref[...] = grad_ref[...]
+    )(packed, dqkv, unit_t, full_qkv, tokens, odd_tokens, d_mixed, mixed, vectors, sums)
+
+
+def finish_kernel(
+    mixed_even, mixed_odd, grad_even, grad_odd, q_ref, r_ref, mixed, grad, g_qkv, g_out, g_in, g_back, *lines
+):
+    block = mixed_even.shape[0]
+    mixed[:block] = mixed_even[...]
+    mixed[block:] = mixed_odd[...]
+    grad[:block] = grad_even[...]
+    grad[block:] = grad_odd[...]
 
     @pl.when(pl.program_id(0) == 0)
     def _():
@@ -1034,10 +1167,11 @@
             line[...] = small[i, :SHARD]
 
 
-def finish(token_grad, q_part, r_part):
-    rows, width = token_grad.shape
-    pieces = 4
-    by_rows = pl.BlockSpec((rows // pieces, width), lambda i: (i, 0))
+def finish(mixed, mixed_odd, grad, grad_odd, q_part, r_part, slots):
+    rows, width = mixed.shape
+    block = rows // slots
+    single = pl.BlockSpec((block, width), lambda i: (i, 0))
+    double = pl.BlockSpec((2 * block, width), lambda i: (i, 0))
 
     def whole(shape):
         return pl.BlockSpec(shape, lambda i: (0,) * len(shape))
@@ -1045,27 +1179,46 @@
     shapes = [(SHARD, 3 * width)] + [(SHARD, width)] * 3 + [(SHARD,)] * 9
     return pl.pallas_call(
         finish_kernel,
-        grid=(pieces,),
-        out_shape=[jax.ShapeDtypeStruct(token_grad.shape, bf16)]
+        grid=(slots // 2,),
+        out_shape=[jax.ShapeDtypeStruct((rows, width), bf16)] * 2
         + [jax.ShapeDtypeStruct(s, f32) for s in shapes],
-        in_specs=[by_rows, whole(q_part.shape), whole(r_part.shape)],
-        out_specs=[by_rows] + [whole(s) for s in shapes],
-    )(token_grad, q_part, r_part)
+        in_specs=[single] * 4 + [whole(q_part.shape), whole(r_part.shape)],
+        out_specs=[double] * 2 + [whole(s) for s in shapes],
+    )(mixed, mixed_odd, grad, grad_odd, q_part, r_part)
 
 
 def on_one_plan(tokens, mol_len, cotangent, vectors, w_qkv, w_out, w_in, w_back):
     slots = mol_len.shape[0]
     small = jnp.pad(jnp.stack(vectors), ((0, 16 - len(vectors)), (0, 128 - SHARD)))
-    qkv, unit_t, full_qkv, full_out, full_in, full_back, lines = gather_and_project(
-        small, w_qkv, w_out, w_in, w_back, tokens, slots
+    (
+        qkv,
+        unit_t,
+        full_qkv,
+        full_out,
+        full_in,
+        full_back,
+        odd_tokens,
+        odd_cotangent,
+        lines,
+        lengths,
+    ) = gather_and_project(mol_len, small, w_qkv, w_out, w_in, w_back, tokens, cotangent)
+    mixed, d_mixed, dqkv, sums, packed = middle(
+        lengths,
+        qkv,
+        (tokens, odd_tokens),
+        (cotangent, odd_cotangent),
+        full_out,
+        full_in,
+        full_back,
+        lines,
+        True,
     )
-    mixed_out, d_mixed, dqkv, sums, packed = middle(
-        mol_len, qkv, tokens, cotangent, full_out, full_in, full_back, lines, True
+    grad, grad_odd, mixed_odd, q_part, r_part = scatter(
+        packed, dqkv, unit_t, full_qkv, tokens, odd_tokens, d_mixed, mixed, lines, sums
     )
-    token_grad, q_part, r_part = scatter(
-        packed, dqkv, unit_t, full_qkv, tokens, d_mixed, lines, sums
+    mixed_out, token_grad, g_qkv, g_out, g_in, g_back, *small = finish(
+        mixed, mixed_odd, grad, grad_odd, q_part, r_part, slots
     )
-    token_grad, g_qkv, g_out, g_in, g_back, *small = finish(token_grad, q_part, r_part)
     return mixed_out, token_grad, small, g_qkv, g_out, g_in, g_back
 
 
@@ -1087,7 +1240,15 @@
     qkv = (qkv + jnp.concatenate([lines[2], jnp.zeros_like(lines[2]), lines[3]])).astype(bf16)
     qkv = qkv.reshape(slots, rows // slots, 3 * width).transpose(0, 2, 1)
     mixed_out, d_mixed, dqkv, sums, g_out, g_in, g_back = middle(
-        mol_len, qkv, tokens, cotangent, full_out, full_in, full_back, lines, False
+        jnp.broadcast_to(mol_len[:, None], (slots, 128)),
+        qkv,
+        (tokens, tokens),
+        (cotangent, cotangent),
+        full_out,
+        full_in,
+        full_back,
+        lines,
+        False,
     )
     g_qkv = jnp.einsum("rf,dr->fd", normed, dqkv, preferred_element_type=f32)
     d_normed = jnp.einsum("dr,fd->rf", dqkv, full_qkv, preferred_element_type=f32)

time: 199 us -> 200 us (level); the launches traced: 200 us -> 198 us
  Pallas kernels: 197 us -> 195 us
    pallas_call x1, Pallas kernels: 75.6 us -> 46.2 us  [middle(): pl.pallas_call(functools.partial(middle_kernel, packed, width // HEADS),...]
    pallas_call x2, Pallas kernels: 55.3 us -> 81.5 us  [the longest x1 75.2 us: scatter(): pl.pallas_call(scatter_kernel, out_shape=[jax.ShapeDtypeStruct((rows // 2...]
where the time goes in v3:
time: 200 us; the launch traced here: 198 us
  Pallas kernels  195 us (98%)
  local copies, waits for them, and re-layouts  2.07 us (1%)
    pallas_call x1, Pallas kernels, scatter(): pl.pallas_call(scatter_kernel, out_shape=[jax.ShapeDtypeStruct((rows // 2...  75.2 us
    pallas_call x1, Pallas kernels, gather_and_project(): pl.pallas_call(gather_kernel, out_shape=[jax.ShapeDtypeStruct((slots, wid...  67.7 us
    pallas_call x1, Pallas kernels, middle(): pl.pallas_call(functools.partial(middle_kernel, packed, width // HEADS),...  46.2 us
    pallas_call x1, Pallas kernels, finish(): pl.pallas_call(finish_kernel, grid=(slots // 2,), out_shape=[jax.ShapeDty...  6.33 us

profile of v3, /device:TPU:0, one launch (start us, length us, event | category | flops | bytes accessed | tf_op | source)
XLA Modules:
  0.0 198.4 jit_solution(8053566149941834418)
XLA Ops:
  0.6 1.5 stack.39
  2.1 0.6 pad.4.small_ref
  2.7 67.7 %shard_map.271 = (bf16[8,2304,256]{2,1,0:T(8,128)(2,1)}, bf16[768,2048]{1,0:T(8,128)(2,1)}, bf16[768,2304]{1,0:T(8,128)(2,1)}, bf16[768,768]{1,0:T(8,128)(2,1)},...) custom-call(s32[8]{0:T(128)} %len_ref.1, ...), custom_call_target="tpu_custom_call" | custom-call | tf_op jit(solution)/shard_map/pallas_call | solution.py:464
  70.5 46.2 %shard_map.272 = (bf16[2048,768]{1,0:T(8,128)(2,1)}, f32[2048,768]{1,0:T(8,128)}, bf16[2304,2048]{1,0:T(8,128)(2,1)}, f32[5,8,768]{2,1,0:T(8,128)}, bf16[32,48,1152]{2,1,0:T(8,128)(2,1)}) custom-call(s32[8,128]{1,0:T(8,128)} %get-tuple-element.50.len_ref, bf16[8,2304,256]{2,1,0:T(8,128)(2,1)} %get-tuple-element.51.qkv_ref, bf16[2048,768]{1,0:T(8,128)(2,1)} %tok_hbm.1, ...), custom_call_target="tpu_custom_call" | custom-call | tf_op jit(solution)/shard_map/pallas_call | solution.py:765
  116.7 75.2 %shard_map.273 = (bf16[1024,768]{1,0:T(8,128)(2,1)}, bf16[1024,768]{1,0:T(8,128)(2,1)}, bf16[1024,768]{1,0:T(8,128)(2,1)}, f32[48,1280]{1,0:T(8,128)}, f32[48,1152]{1,0:T(8,128)}) custom-call(bf16[32,48,1152]{2,1,0:T(8,128)(2,1)} %get-tuple-element.59.sr_hbm, bf16[2304,2048]{1,0:T(8,128)(2,1)} %get-tuple-element.60.dqkv_hbm, ...), custom_call_target="tpu_custom_call" | custom-call | tf_op jit(solution)/shard_map/pallas_call | solution.py:1111
  191.9 6.3 %shard_map.274 = (bf16[2048,768]{1,0:T(8,128)(2,1)}, bf16[2048,768]{1,0:T(8,128)(2,1)}, f32[24,2304]{1,0:T(8,128)}, f32[24,768]{1,0:T(8,128)}, f32[24,768]{1,0:T...) custom-call(bf16[2048,768]{1,0:T(8,128)(2,1)} %get-tuple-element.58., ...), custom_call_target="tpu_custom_call" | custom-call | tf_op jit(solution)/shard_map/pallas_call | solution.py:1180

commit v4 on v3

--- a/solution.py
+++ b/solution.py
@@ -21,6 +21,7 @@
 CHIPS = 4 * PLANES
 DEVICES = 2 * CHIPS
 SHARD = 24
+VECTORS = 9
 
 
 def dot(left, right, left_dim, right_dim):
@@ -78,7 +79,15 @@
 
 def gather_kernel(
     len_ref,
-    small_ref,
+    *refs,
+):
+    lines, refs = refs[:VECTORS], refs[VECTORS:]
+    gather_body(len_ref, lines, *refs)
+
+
+def gather_body(
+    len_ref,
+    lines,
     wq_ref,
     wo_ref,
     wi_ref,
@@ -127,10 +136,13 @@
     mine, theirs = at.c * CHIPS, (1 - at.c) * CHIPS
     slabs = ((gq, 0, 384), (gq, 384, 384), (gq, 768, 512), (gr, 0, 640), (gr, 640, 512))
 
+    small = [line[...].astype(f32).reshape(1, SHARD) for line in lines]
+    small = jnp.concatenate(small + [jnp.zeros((2 * SHARD - VECTORS, SHARD), f32)], axis=0)
+    small = jnp.concatenate([small, jnp.zeros((2 * SHARD, 128 - SHARD), f32)], axis=1).astype(bf16)
     gq[own] = jnp.concatenate(
         [
             jnp.concatenate([wq_ref[:, :half_q], wq_ref[:, half_q:]], axis=0),
-            jnp.concatenate([small_ref[...], jnp.zeros((2 * SHARD - 16, 128), bf16)], axis=0),
+            small,
         ],
         axis=1,
     )
@@ -453,7 +465,7 @@
         copy.wait()
 
 
-def gather_and_project(mol_len, small, w_qkv, w_out, w_in, w_back, tokens, cotangent):
+def gather_and_project(mol_len, vectors, w_qkv, w_out, w_in, w_back, tokens, cotangent):
     slots = mol_len.shape[0]
     rows, width = tokens.shape
     block = rows // slots
@@ -475,7 +487,7 @@
             jax.ShapeDtypeStruct((16, width), f32),
             jax.ShapeDtypeStruct((slots, 128), jnp.int32),
         ],
-        in_specs=[pl.BlockSpec(memory_space=pltpu.SMEM)] + [vmem] * 6 + [anywhere],
+        in_specs=[pl.BlockSpec(memory_space=pltpu.SMEM)] + [vmem] * (VECTORS + 5) + [anywhere],
         out_specs=[anywhere] * 8 + [vmem] * 2,
         scratch_shapes=[
             pltpu.VMEM((DEVICES, 2 * SHARD, wide // 2 + 128), bf16),
@@ -502,7 +514,7 @@
         compiler_params=pltpu.CompilerParams(
             collective_id=0, has_side_effects=True, vmem_limit_bytes=60 * MIB
         ),
-    )(mol_len, small, w_qkv, w_out, w_in, w_back, tokens, cotangent)
+    )(mol_len, *vectors, w_qkv, w_out, w_in, w_back, tokens, cotangent)
 
 
 def middle_kernel(
@@ -611,36 +623,76 @@
         live = (lax.broadcasted_iota(jnp.int32, (size, 1), 0) < length).astype(f32)
         out_bias, gain, shift = vec_ref[4:5], vec_ref[5:6], vec_ref[6:7]
         in_bias, back_bias = vec_ref[7:8], vec_ref[8:9]
-        x = tok_ref[:size].astype(f32)
-        dy = cot_ref[:size].astype(f32)
-        ctx_t = ctx_s[:, :size].astype(bf16)
-        attn = dot(ctx_t.T, wout_ref[...], 1, 0) + out_bias
-        mixed = x + live * attn
-        unit, factor = normalize(mixed)
-        normed = (unit * gain + shift).astype(bf16)
-        pre = dot(normed, win_ref[...], 1, 0) + in_bias
-        cdf = 0.5 * (1.0 + lax.erf(pre * 0.7071067811865476))
-        act = (pre * cdf).astype(bf16)
-        slope = cdf + pre * jnp.exp(-0.5 * pre * pre) * 0.3989422804014327
-        branch = dot(act, wback_ref[...], 1, 0) + back_bias
-        mixed_ref[:size] = (mixed + live * branch).astype(bf16)
-        d_ffn = live * dy
+
+        strips = [slice(c, c + 256) for c in range(0, width, 256)]
+
+        def row_mean(parts):
+            return sum(jnp.sum(p, axis=1, keepdims=True) for p in parts) * (1.0 / width)
+
+        def join(parts):
+            return jnp.concatenate(parts, axis=1)
+
+        d_ffn = cot_ref[:size].astype(f32) * live
         gvec_ref[4] += fold_rows(d_ffn)
         d_ffn = d_ffn.astype(bf16)
-        gback_ref[...] += dot(act.T, d_ffn, 1, 0)
-        d_act = dot(d_ffn, wback_ref[...], 1, 1)
-        d_pre = (d_act * slope).astype(bf16)
-        gvec_ref[3] += fold_rows(d_pre.astype(f32))
-        gin_ref[...] += dot(normed.T, d_pre, 1, 0)
-        d_normed = dot(d_pre, win_ref[...], 1, 1)
-        gvec_ref[1] += fold_rows(d_normed * unit)
-        gvec_ref[2] += fold_rows(d_normed)
-        d_mixed = dy + norm_backward(d_normed, gain, unit, factor)
-        dmix_ref[:size] = d_mixed
-        d_attn = (live * d_mixed).astype(bf16)
-        gvec_ref[0] += fold_rows(d_attn.astype(f32))
-        gout_ref[...] += dot(ctx_t, d_attn, 1, 0)
-        dctx_s[:, :size] = dot(wout_ref[...], d_attn, 1, 1).astype(bf16)
+        ctx_t = ctx_s[:, :size].astype(bf16)
+        ctx = ctx_t.T
+        mixed = []
+        for c in strips:
+            attn = dot(ctx, wout_ref[:, c], 1, 0) + out_bias[:, c]
+            mixed.append(tok_ref[:size, c].astype(f32) + live * attn)
+        d_act = [dot(d_ffn, wback_ref[c], 1, 1) for c in strips[:1]]
+        mean = row_mean(mixed)
+        centred = [m - mean for m in mixed]
+        factor = lax.rsqrt(row_mean([v * v for v in centred]) + eps)
+        unit = [v * factor for v in centred]
+        normed = join(
+            [(u * gain[:, c] + shift[:, c]).astype(bf16) for u, c in zip(unit, strips)]
+        )
+        act, d_pre = [], []
+
+        def project(c):
+            return dot(normed, win_ref[:, c], 1, 0) + in_bias[:, c]
+
+        ahead_pre = [project(strips[0])]
+        for i, c in enumerate(strips):
+            if i + 1 < len(strips):
+                ahead_pre.append(project(strips[i + 1]))
+                d_act.append(dot(d_ffn, wback_ref[strips[i + 1]], 1, 1))
+            pre = ahead_pre[i]
+            cdf = 0.5 * (1.0 + lax.erf(pre * 0.7071067811865476))
+            act.append((pre * cdf).astype(bf16))
+            slope = cdf + pre * jnp.exp(-0.5 * pre * pre) * 0.3989422804014327
+            low = (d_act[i] * slope).astype(bf16)
+            gvec_ref[3, :, c] += fold_rows(low.astype(f32))
+            d_pre.append(low)
+        act, d_pre = join(act), join(d_pre)
+        d_normed = [dot(d_pre, win_ref[c], 1, 1) for c in strips]
+        for m, c in zip(mixed, strips):
+            branch = dot(act, wback_ref[:, c], 1, 0) + back_bias[:, c]
+            mixed_ref[:size, c] = (m + live * branch).astype(bf16)
+        act_t, normed_t = act.T, normed.T
+        e = []
+        for i, c in enumerate(strips):
+            gback_ref[:, c] += dot(act_t, d_ffn[:, c], 1, 0)
+            gvec_ref[1, :, c] += fold_rows(d_normed[i] * unit[i])
+            gvec_ref[2, :, c] += fold_rows(d_normed[i])
+            e.append(d_normed[i] * gain[:, c])
+        mean = row_mean(e)
+        inner = row_mean([v * u for v, u in zip(e, unit)])
+        d_attn = []
+        for i, c in enumerate(strips):
+            gin_ref[:, c] += dot(normed_t, d_pre[:, c], 1, 0)
+            d_mixed = cot_ref[:size, c].astype(f32) + factor * (e[i] - mean - unit[i] * inner)
+            dmix_ref[:size, c] = d_mixed
+            low = (live * d_mixed).astype(bf16)
+            gvec_ref[0, :, c] += fold_rows(low.astype(f32))
+            d_attn.append(low)
+        d_attn = join(d_attn)
+        for c in strips:
+            dctx_s[c, :size] = dot(wout_ref[c], d_attn, 1, 1).astype(bf16)
+        for c in strips:
+            gout_ref[:, c] += dot(ctx_t, d_attn[:, c], 1, 0)
 
         behind = 3 if size > 128 else 6
 
@@ -1189,7 +1241,6 @@
 
 def on_one_plan(tokens, mol_len, cotangent, vectors, w_qkv, w_out, w_in, w_back):
     slots = mol_len.shape[0]
-    small = jnp.pad(jnp.stack(vectors), ((0, 16 - len(vectors)), (0, 128 - SHARD)))
     (
         qkv,
         unit_t,
@@ -1201,7 +1252,7 @@
         odd_cotangent,
         lines,
         lengths,
-    ) = gather_and_project(mol_len, small, w_qkv, w_out, w_in, w_back, tokens, cotangent)
+    ) = gather_and_project(mol_len, vectors, w_qkv, w_out, w_in, w_back, tokens, cotangent)
     mixed, d_mixed, dqkv, sums, packed = middle(
         lengths,
         qkv,

time: 200 us -> 189 us (0.945)
  Pallas kernels: 195 us -> 188 us
  local copies, waits for them, and re-layouts: 2.07 us -> 0 us
    pallas_call x1, Pallas kernels: 75.2 us -> 105 us  [scatter(): pl.pallas_call(scatter_kernel, out_shape=[jax.ShapeDtypeStruct((rows // 2...]
    pallas_call x1, Pallas kernels: 46.2 us -> 22.6 us  [middle(): pl.pallas_call(functools.partial(middle_kernel, packed, width // HEADS),...]
    pallas_call x1, Pallas kernels: 67.7 us -> 53.5 us  [gather_and_project(): pl.pallas_call(gather_kernel, out_shape=[jax.ShapeDtypeStruct((slots, wid...]
where the time goes in v4:
time: 189 us
  Pallas kernels  188 us (99%)
    pallas_call x1, Pallas kernels, scatter(): pl.pallas_call(scatter_kernel, out_shape=[jax.ShapeDtypeStruct((rows // 2...  105 us
    pallas_call x1, Pallas kernels, gather_and_project(): pl.pallas_call(gather_kernel, out_shape=[jax.ShapeDtypeStruct((slots, wid...  53.5 us
    pallas_call x1, Pallas kernels, middle(): pl.pallas_call(functools.partial(middle_kernel, packed, width // HEADS),...  22.6 us
    pallas_call x1, Pallas kernels, finish(): pl.pallas_call(finish_kernel, grid=(slots // 2,), out_shape=[jax.ShapeDty...  6.33 us

profile of v4, /device:TPU:0, one launch (start us, length us, event | category | flops | bytes accessed | tf_op | source)
XLA Modules:
  0.0 188.7 jit_solution(7363646374383119654)
XLA Ops:
  0.7 53.5 %shard_map.271 = (bf16[8,2304,256]{2,1,0:T(8,128)(2,1)}, bf16[768,2048]{1,0:T(8,128)(2,1)}, bf16[768,2304]{1,0:T(8,128)(2,1)}, bf16[768,768]{1,0:T(8,128)(2,1)},...) custom-call(s32[8]{0:T(128)} %len_ref.1, ...), custom_call_target="tpu_custom_call" | custom-call | tf_op jit(solution)/shard_map/pallas_call | solution.py:476
  54.2 22.6 %shard_map.272 = (bf16[2048,768]{1,0:T(8,128)(2,1)}, f32[2048,768]{1,0:T(8,128)}, bf16[2304,2048]{1,0:T(8,128)(2,1)}, f32[5,8,768]{2,1,0:T(8,128)}, bf16[32,48,1152]{2,1,0:T(8,128)(2,1)}) custom-call(s32[8,128]{1,0:T(8,128)} %get-tuple-element.50.len_ref, bf16[8,2304,256]{2,1,0:T(8,128)(2,1)} %get-tuple-element.51.qkv_ref, bf16[2048,768]{1,0:T(8,128)(2,1)} %tok_hbm.1, ...), custom_call_target="tpu_custom_call" | custom-call | tf_op jit(solution)/shard_map/pallas_call | solution.py:817
  76.8 105.3 %shard_map.273 = (bf16[1024,768]{1,0:T(8,128)(2,1)}, bf16[1024,768]{1,0:T(8,128)(2,1)}, bf16[1024,768]{1,0:T(8,128)(2,1)}, f32[48,1280]{1,0:T(8,128)}, f32[48,1152]{1,0:T(8,128)}) custom-call(bf16[32,48,1152]{2,1,0:T(8,128)(2,1)} %get-tuple-element.59.sr_hbm, bf16[2304,2048]{1,0:T(8,128)(2,1)} %get-tuple-element.60.dqkv_hbm, ...), custom_call_target="tpu_custom_call" | custom-call | tf_op jit(solution)/shard_map/pallas_call | solution.py:1163
  182.1 6.3 %shard_map.274 = (bf16[2048,768]{1,0:T(8,128)(2,1)}, bf16[2048,768]{1,0:T(8,128)(2,1)}, f32[24,2304]{1,0:T(8,128)}, f32[24,768]{1,0:T(8,128)}, f32[24,768]{1,0:T...) custom-call(bf16[2048,768]{1,0:T(8,128)(2,1)} %get-tuple-element.58., ...), custom_call_target="tpu_custom_call" | custom-call | tf_op jit(solution)/shard_map/pallas_call | solution.py:1232
